TPU v7x, 32 devices: a whole 2x2x4 slice. The times are simulated.
32 devices in a mesh: dp: 8 (over z, x), ctx: 4 (over y, core).
Axes of the slice: x: 2, y: 2, z: 4, core: 2. Of those that a mesh axis runs over, the one named last changes fastest.
Arguments:
- hidden: bfloat16 [2, 8192, 1024], P(None, ('dp', 'ctx')), may hold values from -6 to 6
- cotangent: bfloat16 [2, 8192, 1024], P(None, ('dp', 'ctx')), may hold values from -6 to 6
- seq_lengths: int32 [8, 2, 1], P('dp'), may hold values from 512 to 1024, as said below
- norm_gain: bfloat16 [1024], P(('dp', 'ctx')), may hold values from 0.099609375 to 1.8984375
- in_proj: bfloat16 [1024, 3352], P(('dp', 'ctx')), may hold values from -1 to 1
- conv_weight: bfloat16 [4, 1792], P(None, ('dp', 'ctx')), may hold values from -3 to 3
- conv_bias: bfloat16 [1792], P(('dp', 'ctx')), may hold values from -3 to 3
- gate_gain: bfloat16 [1536], P(('dp', 'ctx')), may hold values from 0.099609375 to 1.8984375
- out_proj: bfloat16 [1536, 1024], P(('dp', 'ctx')), may hold values from -0.15625 to 0.15625
- q_proj: bfloat16 [1024, 512], P(('dp', 'ctx')), may hold values from -0.1875 to 0.1875
- kv_proj: bfloat16 [1024, 256], P(('dp', 'ctx')), may hold values from -0.1875 to 0.1875
- o_proj: bfloat16 [512, 1024], P(('dp', 'ctx')), may hold values from -2 to 2
- ff_gain: bfloat16 [1024], P(('dp', 'ctx')), may hold values from 0.099609375 to 1.8984375
- gate_up: bfloat16 [1024, 4096], P(('dp', 'ctx')), may hold values from -0.1875 to 0.1875
- down_proj: bfloat16 [2048, 1024], P(('dp', 'ctx')), may hold values from -0.125 to 0.125
- a_log: float32 [24], replicated, may hold values from -3.5 to 0.5
- dt_bias: float32 [24], replicated, may hold values from -4.5 to -2.5
- skip_scale: float32 [24], replicated, may hold values from 0.25 to 1
Outputs:
- layer_out: bfloat16 [2, 8192, 1024], P(None, ('dp', 'ctx'))
- grad_hidden: bfloat16 [2, 8192, 1024], P(None, ('dp', 'ctx'))
- grad_norm_gain: float32 [1024], P(('dp', 'ctx'))
- grad_in_proj: float32 [1024, 3352], P(('dp', 'ctx'))
- grad_conv_weight: float32 [4, 1792], P(None, ('dp', 'ctx'))
- grad_conv_bias: float32 [1792], P(('dp', 'ctx'))
- grad_gate_gain: float32 [1536], P(('dp', 'ctx'))
- grad_out_proj: float32 [1536, 1024], P(('dp', 'ctx'))
- grad_q_proj: float32 [1024, 512], P(('dp', 'ctx'))
- grad_kv_proj: float32 [1024, 256], P(('dp', 'ctx'))
- grad_o_proj: float32 [512, 1024], P(('dp', 'ctx'))
- grad_ff_gain: float32 [1024], P(('dp', 'ctx'))
- grad_gate_up: float32 [1024, 4096], P(('dp', 'ctx'))
- grad_down_proj: float32 [2048, 1024], P(('dp', 'ctx'))
- grad_a_log: float32 [24], replicated
- grad_dt_bias: float32 [24], replicated
- grad_skip_scale: float32 [24], replicated
Inputs may be any that keep to these rules, and one draw needn't show every extreme that they name: `seq_lengths`: in each group and micro-batch the given sequences come first, then zeros; there is at least one sequence; a nonzero length lies between 512 and 1024 and is a multiple of the number of devices along ctx; the lengths of one group and micro-batch sum to at most 1024, and some group and micro-batch reach that sum.
All inputs are finite; a program needn't handle non-finite values.
Results may differ from a plain program's by a relative error of at most 0.038.
Values may be sent and summed in bfloat16 or wider, within the bound.
A program may use at most 256 MiB of HBM per device.

v0:
```python
import jax
import jax.numpy as jnp
from jax import lax
from jax.sharding import PartitionSpec as P

MH = 24
HP = 64
NS = 128
CONV = 4
AH = 8
KVH = 2
AD = 64
MICRO = 2
DI = 1536
XC = 1792
QD = 512
KD = 128


EPSILON = 1e-05
HIGHEST = lax.Precision.HIGHEST
MASKED = -1e30


def from_behind(block, axis, distance):
    devices = range(lax.axis_size(axis))
    route = [(i - distance, i) for i in devices if i - distance in devices]
    return lax.ppermute(block, axis, route)


def rms_scale(signal, scale):
    return signal * lax.rsqrt(jnp.mean(signal * signal, axis=-1, keepdims=True) + EPSILON) * scale


def swiglu(joined):
    half_cols = joined.shape[1] // 2
    return jax.nn.silu(joined[:, :half_cols]) * joined[:, half_cols:]


def plain_dot(first_arg, second_arg):
    return jnp.dot(first_arg, second_arg, preferred_element_type=jnp.float32)


def left_dot(first_arg, second_arg):
    return lax.dot_general(
        first_arg, second_arg, (((0,), (0,)), ((), ())), preferred_element_type=jnp.float32
    )


def right_dot(first_arg, second_arg):
    return lax.dot_general(
        first_arg, second_arg, (((1,), (1,)), ((), ())), preferred_element_type=jnp.float32
    )


def row_layout(span_len, row_count, ctx_place):
    seq_ends = jnp.cumsum(span_len)
    filled = seq_ends[-1]
    local_row = jnp.arange(row_count, dtype=jnp.int32)
    passed = local_row[:, None] >= seq_ends[None, :]
    segment = jnp.sum(passed.astype(jnp.int32), axis=1)
    start_row = jnp.sum(jnp.where(passed, span_len[None, :], 0), axis=1)
    slot_count = span_len.shape[0]
    owner = segment[:, None] == jnp.arange(slot_count, dtype=jnp.int32)[None, :]
    extent = jnp.sum(jnp.where(owner, span_len[None, :], 0), axis=1) + jnp.where(
        segment == slot_count, row_count - filled, 0
    )
    offset = local_row - start_row
    position = ctx_place * extent + offset
    alive_row = (local_row < filled).astype(jnp.float32)
    return (segment, offset, extent, position, alive_row, seq_ends)


def mamba_local(
    xbc_val, raw_step, tail_val, w_conv_val, b_conv_val, log_a, bias_dt, skip_val, segment, offset
):
    row_count = xbc_val.shape[0]
    tail_len = CONV - 1
    slot_count = tail_val.shape[0] // tail_len
    convolved = b_conv_val[None, :] + w_conv_val[tail_len][None, :] * xbc_val
    tail_seat = jnp.arange(slot_count * tail_len, dtype=jnp.int32)
    for shift_by in range(1, CONV):
        shifted = jnp.concatenate(
            [jnp.zeros((shift_by, xbc_val.shape[1]), jnp.float32), xbc_val[: row_count - shift_by]],
            axis=0,
        )
        inside = (offset >= shift_by)[:, None]
        choose = (
            (segment[:, None] == tail_seat[None, :] // tail_len)
            & (tail_seat[None, :] % tail_len == offset[:, None] + tail_len - shift_by)
            & (offset < shift_by)[:, None]
        )
        carried = jnp.dot(choose.astype(jnp.float32), tail_val, precision=HIGHEST)
        convolved = (
            convolved
            + (jnp.where(inside, shifted, 0.0) + carried) * w_conv_val[tail_len - shift_by][None, :]
        )
    activated = jax.nn.silu(convolved)
    values = activated[:, :DI].reshape(row_count, MH, HP)
    b_in = activated[:, DI : DI + NS]
    c_out = activated[:, DI + NS :]
    step_size = jax.nn.softplus(raw_step + bias_dt[None, :])
    log_decay = -step_size * jnp.exp(log_a)[None, :]
    scaled = values * step_size[:, :, None]
    member = (segment[:, None] == jnp.arange(slot_count + 1, dtype=jnp.int32)[None, :]).astype(
        jnp.float32
    )
    seg_sum = jnp.dot(member.T, log_decay, precision=HIGHEST)
    lower_tri = jnp.tril(jnp.ones((slot_count + 1, slot_count + 1), jnp.float32), -1)
    earlier_sum = jnp.dot(lower_tri, seg_sum, precision=HIGHEST)
    within = jnp.cumsum(log_decay, axis=0) - jnp.dot(member, earlier_sum, precision=HIGHEST)
    qblock = min(512, row_count)
    all_rows = jnp.arange(row_count, dtype=jnp.int32)

    def one_block(block_index):
        start_at = block_index * qblock
        own_rows = start_at + jnp.arange(qblock, dtype=jnp.int32)
        allowed = (segment[:, None] == segment[None, :]) & (own_rows[:, None] >= all_rows[None, :])
        decay_mat = jnp.where(
            allowed[:, :, None],
            jnp.exp(jnp.minimum(within[:, None, :] - within[None, :, :], 0.0)),
            0.0,
        )
        inner_cb = jnp.dot(c_out, b_in.T, precision=HIGHEST)
        return jnp.einsum(
            "tsh,shp->thp", decay_mat * inner_cb[:, :, None], scaled, precision=HIGHEST
        )

    local_out = lax.map(
        jax.checkpoint(one_block), jnp.arange(row_count // qblock, dtype=jnp.int32)
    ).reshape(row_count, MH, HP)
    local_out = local_out + skip_val[None, :, None] * values
    to_end = jnp.exp(jnp.minimum(jnp.dot(member, seg_sum, precision=HIGHEST) - within, 0.0))
    weighted = jnp.einsum("ts,th->tsh", member[:, :slot_count], to_end, precision=HIGHEST)
    end_state = jnp.einsum("tsh,thp,tn->shpn", weighted, scaled, b_in, precision=HIGHEST)
    span_decay = jnp.exp(seg_sum[:slot_count])
    return (local_out.reshape(row_count, DI), end_state, span_decay, c_out, jnp.exp(within))


def mamba_finish(local_out, c_out, from_start, state_in, gate_input, gate_scale, segment):
    row_count = local_out.shape[0]
    slot_count = state_in.shape[0]
    member = (segment[:, None] == jnp.arange(slot_count, dtype=jnp.int32)[None, :]).astype(
        jnp.float32
    )
    readout = jnp.einsum("tn,shpn->sthp", c_out, state_in, precision=HIGHEST)
    carried = (
        jnp.einsum("ts,sthp->thp", member, readout, precision=HIGHEST) * from_start[:, :, None]
    )
    full_out = local_out + carried.reshape(row_count, DI)
    return rms_scale(full_out * jax.nn.silu(gate_input), gate_scale)


def body(
    hidden,
    cotangent,
    seq_lengths,
    norm_gain,
    in_proj,
    conv_weight,
    conv_bias,
    gate_gain,
    out_proj,
    q_proj,
    kv_proj,
    o_proj,
    ff_gain,
    gate_up,
    down_proj,
    a_log,
    dt_bias,
    skip_scale,
):
    ctx_count = lax.axis_size("ctx")
    ctx_place = lax.axis_index("ctx")
    row_count = hidden.shape[1]
    groups = AH // KVH
    scale_qk = AD ** (-0.5)
    head_totals = (jnp.zeros_like(a_log), jnp.zeros_like(dt_bias), jnp.zeros_like(skip_scale))
    totals = None
    outs_list = []
    grads_list = []
    for micro_index in range(MICRO):
        gathered = (
            lax.all_gather(norm_gain, ("dp", "ctx"), axis=0, tiled=True),
            lax.all_gather(in_proj, ("dp", "ctx"), axis=0, tiled=True),
            lax.all_gather(conv_weight, ("dp", "ctx"), axis=1, tiled=True),
            lax.all_gather(conv_bias, ("dp", "ctx"), axis=0, tiled=True),
            lax.all_gather(gate_gain, ("dp", "ctx"), axis=0, tiled=True),
            lax.all_gather(out_proj, ("dp", "ctx"), axis=0, tiled=True),
            lax.all_gather(q_proj, ("dp", "ctx"), axis=0, tiled=True),
            lax.all_gather(kv_proj, ("dp", "ctx"), axis=0, tiled=True),
            lax.all_gather(o_proj, ("dp", "ctx"), axis=0, tiled=True),
            lax.all_gather(ff_gain, ("dp", "ctx"), axis=0, tiled=True),
            lax.all_gather(gate_up, ("dp", "ctx"), axis=0, tiled=True),
            lax.all_gather(down_proj, ("dp", "ctx"), axis=0, tiled=True),
        )
        g_norm, w_in, w_conv, b_conv, g_gate, w_out, w_q, w_kv, w_o, g_ff, w_gu, w_down = gathered
        if totals is None:
            totals = tuple((jnp.zeros(weight.shape, jnp.float32) for weight in gathered))
        span_len = seq_lengths[0, micro_index] // ctx_count
        segment, offset, extent, position, alive_row, seq_ends = row_layout(
            span_len, row_count, ctx_place
        )
        x_in = hidden[micro_index].astype(jnp.float32)
        normed, norm_pull = jax.vjp(rms_scale, x_in, g_norm.astype(jnp.float32))
        normed_b = normed.astype(jnp.bfloat16)
        mixed = plain_dot(normed_b, w_in).astype(jnp.bfloat16)
        query_b = plain_dot(normed_b, w_q).astype(jnp.bfloat16)
        keyval_b = plain_dot(normed_b, w_kv).astype(jnp.bfloat16)
        tail_targets = (
            seq_ends[:, None] - (CONV - 1) + jnp.arange(CONV - 1, dtype=jnp.int32)[None, :]
        ).reshape(-1)
        tail_pick = (
            tail_targets[:, None] == jnp.arange(row_count, dtype=jnp.int32)[None, :]
        ).astype(jnp.float32)
        tail_rows = plain_dot(tail_pick.astype(jnp.bfloat16), mixed[:, DI : DI + XC]).astype(
            jnp.bfloat16
        )
        tail_in = from_behind(tail_rows, "ctx", 1)

        def mamba_front(
            xbc_val, raw_step, tail_val, w_conv_val, b_conv_val, log_a, bias_dt, skip_val
        ):
            return mamba_local(
                xbc_val,
                raw_step,
                tail_val,
                w_conv_val,
                b_conv_val,
                log_a,
                bias_dt,
                skip_val,
                segment,
                offset,
            )

        front_out, front_pull = jax.vjp(
            mamba_front,
            mixed[:, DI : DI + XC].astype(jnp.float32),
            mixed[:, DI + XC :].astype(jnp.float32),
            tail_in.astype(jnp.float32),
            w_conv.astype(jnp.float32),
            b_conv.astype(jnp.float32),
            a_log,
            dt_bias,
            skip_scale,
        )
        local_out, end_state, span_decay, c_out, from_start = front_out
        decay_wide = span_decay[:, :, None, None]

        def pass_state(step_index, carry):
            outgoing, received = carry
            received = from_behind(outgoing.astype(jnp.bfloat16), "ctx", 1).astype(outgoing.dtype)
            return (decay_wide * received + end_state, received)

        _, state_in = lax.fori_loop(
            0, ctx_count - 1, pass_state, (end_state, jnp.zeros_like(end_state))
        )

        def mamba_back_end(local_val, c_val, from_val, state_val, gate_val, gain_val):
            return mamba_finish(local_val, c_val, from_val, state_val, gate_val, gain_val, segment)

        mamba_norm, finish_pull = jax.vjp(
            mamba_back_end,
            local_out,
            c_out,
            from_start,
            state_in,
            mixed[:, :DI].astype(jnp.float32),
            g_gate.astype(jnp.float32),
        )
        mamba_norm_b = mamba_norm.astype(jnp.bfloat16)
        mamba_branch = plain_dot(mamba_norm_b, w_out)
        query_heads = query_b.reshape(row_count, KVH, groups, AD)
        key_piece = lax.all_gather(keyval_b, "ctx", axis=0, tiled=True)
        run_max = jnp.full((row_count, KVH, groups), MASKED, jnp.float32)
        piece_rows = key_piece.shape[0]
        key_rows = jnp.arange(piece_rows, dtype=jnp.int32)
        source = key_rows // row_count
        local_key = key_rows % row_count
        key_seg = segment[local_key]
        key_pos = source * extent[local_key] + offset[local_key]
        key_heads = key_piece[:, :KD].reshape(piece_rows, KVH, AD)
        value_heads = key_piece[:, KD:].reshape(piece_rows, KVH, AD)
        score_mat = (
            jnp.einsum("tgjd,sgd->tgjs", query_heads, key_heads, preferred_element_type=jnp.float32)
            * scale_qk
        )
        allowed = (
            (segment[:, None] == key_seg[None, :]) & (position[:, None] >= key_pos[None, :])
        )[:, None, None, :]
        score_mat = jnp.where(allowed, score_mat, MASKED)
        new_max = jnp.maximum(run_max, jnp.max(score_mat, axis=-1))
        weights = jnp.where(allowed, jnp.exp(score_mat - new_max[..., None]), 0.0)
        run_sum = jnp.sum(weights, axis=-1)
        run_acc = jnp.einsum(
            "tgjs,sgd->tgjd",
            weights.astype(jnp.bfloat16),
            value_heads,
            preferred_element_type=jnp.float32,
        )
        run_max, run_sum, run_acc = (new_max, run_sum, run_acc)
        attended = run_acc / run_sum[..., None]
        log_total = run_max + jnp.log(run_sum)
        attended_b = attended.reshape(row_count, QD).astype(jnp.bfloat16)
        attn_branch = plain_dot(attended_b, w_o)
        middle = x_in + mamba_branch + attn_branch
        normed_ff, ff_pull = jax.vjp(rms_scale, middle, g_ff.astype(jnp.float32))
        normed_ff_b = normed_ff.astype(jnp.bfloat16)
        gate_up_b = plain_dot(normed_ff_b, w_gu).astype(jnp.bfloat16)
        activation, act_pull = jax.vjp(swiglu, gate_up_b.astype(jnp.float32))
        activation_b = activation.astype(jnp.bfloat16)
        ff_branch = plain_dot(activation_b, w_down)
        outs_list.append(((middle + ff_branch) * alive_row[:, None]).astype(jnp.bfloat16))
        gathered_back = (
            lax.all_gather(norm_gain, ("dp", "ctx"), axis=0, tiled=True),
            lax.all_gather(in_proj, ("dp", "ctx"), axis=0, tiled=True),
            lax.all_gather(conv_weight, ("dp", "ctx"), axis=1, tiled=True),
            lax.all_gather(conv_bias, ("dp", "ctx"), axis=0, tiled=True),
            lax.all_gather(gate_gain, ("dp", "ctx"), axis=0, tiled=True),
            lax.all_gather(out_proj, ("dp", "ctx"), axis=0, tiled=True),
            lax.all_gather(q_proj, ("dp", "ctx"), axis=0, tiled=True),
            lax.all_gather(kv_proj, ("dp", "ctx"), axis=0, tiled=True),
            lax.all_gather(o_proj, ("dp", "ctx"), axis=0, tiled=True),
            lax.all_gather(ff_gain, ("dp", "ctx"), axis=0, tiled=True),
            lax.all_gather(gate_up, ("dp", "ctx"), axis=0, tiled=True),
            lax.all_gather(down_proj, ("dp", "ctx"), axis=0, tiled=True),
        )
        back_in = gathered_back[1]
        back_out = gathered_back[5]
        back_q = gathered_back[6]
        back_kv = gathered_back[7]
        back_o = gathered_back[8]
        back_gu = gathered_back[10]
        back_down = gathered_back[11]
        d_out = cotangent[micro_index].astype(jnp.float32) * alive_row[:, None]
        d_ff_b = d_out.astype(jnp.bfloat16)
        g_down = left_dot(activation_b, d_ff_b)
        d_act = right_dot(d_ff_b, back_down)
        (d_gate_up,) = act_pull(d_act)
        d_gate_up_b = d_gate_up.astype(jnp.bfloat16)
        g_gu = left_dot(normed_ff_b, d_gate_up_b)
        d_normed_ff = right_dot(d_gate_up_b, back_gu)
        d_mid_part, g_ffgain = ff_pull(d_normed_ff)
        d_mid = d_out + d_mid_part
        d_branch_b = d_mid.astype(jnp.bfloat16)
        g_out = left_dot(mamba_norm_b, d_branch_b)
        g_o = left_dot(attended_b, d_branch_b)
        d_mamba_norm = right_dot(d_branch_b, back_out)
        d_attended_b = (
            right_dot(d_branch_b, back_o).astype(jnp.bfloat16).reshape(row_count, KVH, groups, AD)
        )
        row_delta = jnp.sum(d_attended_b.astype(jnp.float32) * attended, axis=-1)
        every_kv = lax.all_gather(keyval_b, "ctx", axis=0, tiled=True)

        def back_piece(dq_acc, shard_index):
            key_piece = lax.dynamic_slice_in_dim(every_kv, shard_index * row_count, row_count, 0)
            key_pos = shard_index * extent + offset
            key_heads = key_piece[:, :KD].reshape(row_count, KVH, AD)
            value_heads = key_piece[:, KD:].reshape(row_count, KVH, AD)
            score_mat = (
                jnp.einsum(
                    "tgjd,sgd->tgjs", query_heads, key_heads, preferred_element_type=jnp.float32
                )
                * scale_qk
            )
            allowed = (
                (segment[:, None] == segment[None, :]) & (position[:, None] >= key_pos[None, :])
            )[:, None, None, :]
            probs = jnp.exp(jnp.where(allowed, score_mat - log_total[..., None], MASKED))
            d_probs = jnp.einsum(
                "tgjd,sgd->tgjs", d_attended_b, value_heads, preferred_element_type=jnp.float32
            )
            d_score = (probs * (d_probs - row_delta[..., None])).astype(jnp.bfloat16)
            dq_acc = (
                dq_acc
                + jnp.einsum(
                    "tgjs,sgd->tgjd", d_score, key_heads, preferred_element_type=jnp.float32
                )
                * scale_qk
            )
            d_keys = (
                jnp.einsum(
                    "tgjs,tgjd->sgd", d_score, query_heads, preferred_element_type=jnp.float32
                )
                * scale_qk
            )
            d_values = jnp.einsum(
                "tgjs,tgjd->sgd",
                probs.astype(jnp.bfloat16),
                d_attended_b,
                preferred_element_type=jnp.float32,
            )
            return (
                dq_acc,
                jnp.concatenate(
                    [d_keys.reshape(row_count, KD), d_values.reshape(row_count, KD)], axis=1
                ),
            )

        d_query, kv_terms = lax.scan(
            back_piece,
            jnp.zeros((row_count, KVH, groups, AD), jnp.float32),
            jnp.arange(ctx_count, dtype=jnp.int32),
        )
        d_keyval = lax.psum_scatter(
            kv_terms.reshape(ctx_count * row_count, 2 * KD).astype(jnp.bfloat16),
            "ctx",
            scatter_dimension=0,
            tiled=True,
        )
        d_query_b = d_query.reshape(row_count, QD).astype(jnp.bfloat16)
        g_q = left_dot(normed_b, d_query_b)
        g_kv = left_dot(normed_b, d_keyval)
        d_local, d_cout, d_from, d_state_in, d_gate_z, g_gategain = finish_pull(d_mamba_norm)

        def pass_grad(step_index, carry):
            outgoing, received = carry
            received = from_behind(outgoing.astype(jnp.bfloat16), "ctx", -1).astype(outgoing.dtype)
            return (d_state_in + decay_wide * received, received)

        _, d_end_state = lax.fori_loop(
            0, ctx_count - 1, pass_grad, (d_state_in, jnp.zeros_like(d_state_in))
        )
        d_span_decay = jnp.sum(d_end_state * state_in, axis=(2, 3))
        d_xbc, d_raw_step, d_tail, g_conv, g_convbias, g_alog, g_dtbias, g_skip = front_pull(
            (d_local, d_end_state, d_span_decay, d_cout, d_from)
        )
        tail_back = from_behind(d_tail, "ctx", -1)
        d_xbc = d_xbc + jnp.dot(tail_pick.T, tail_back, precision=HIGHEST)
        d_mixed_b = jnp.concatenate([d_gate_z, d_xbc, d_raw_step], axis=1).astype(jnp.bfloat16)
        g_in = left_dot(normed_b, d_mixed_b)
        d_normed = (
            right_dot(d_mixed_b, back_in)
            + right_dot(d_query_b, back_q)
            + right_dot(d_keyval, back_kv)
        )
        d_x_part, g_normgain = norm_pull(d_normed)
        grads_list.append((d_mid + d_x_part).astype(jnp.bfloat16))
        step_grads = (
            g_normgain,
            g_in,
            g_conv,
            g_convbias,
            g_gategain,
            g_out,
            g_q,
            g_kv,
            g_o,
            g_ffgain,
            g_gu,
            g_down,
        )
        totals = tuple((total + grad for total, grad in zip(totals, step_grads)))
        head_totals = (head_totals[0] + g_alog, head_totals[1] + g_dtbias, head_totals[2] + g_skip)
    reduced = (
        lax.psum_scatter(totals[0], ("dp", "ctx"), scatter_dimension=0, tiled=True),
        lax.psum_scatter(totals[1], ("dp", "ctx"), scatter_dimension=0, tiled=True),
        lax.psum_scatter(totals[2], ("dp", "ctx"), scatter_dimension=1, tiled=True),
        lax.psum_scatter(totals[3], ("dp", "ctx"), scatter_dimension=0, tiled=True),
        lax.psum_scatter(totals[4], ("dp", "ctx"), scatter_dimension=0, tiled=True),
        lax.psum_scatter(totals[5], ("dp", "ctx"), scatter_dimension=0, tiled=True),
        lax.psum_scatter(totals[6], ("dp", "ctx"), scatter_dimension=0, tiled=True),
        lax.psum_scatter(totals[7], ("dp", "ctx"), scatter_dimension=0, tiled=True),
        lax.psum_scatter(totals[8], ("dp", "ctx"), scatter_dimension=0, tiled=True),
        lax.psum_scatter(totals[9], ("dp", "ctx"), scatter_dimension=0, tiled=True),
        lax.psum_scatter(totals[10], ("dp", "ctx"), scatter_dimension=0, tiled=True),
        lax.psum_scatter(totals[11], ("dp", "ctx"), scatter_dimension=0, tiled=True),
    )
    head_sum = lax.psum((head_totals[0], head_totals[1], head_totals[2]), ("dp", "ctx"))
    layer_out = jnp.stack(outs_list, axis=0)
    grad_hidden = jnp.stack(grads_list, axis=0)
    return (layer_out, grad_hidden) + tuple(reduced) + tuple(head_sum)


def solution(mesh):
    placed = (
        P(None, ("dp", "ctx"), None),
        P(None, ("dp", "ctx"), None),
        P("dp", None, None),
        P(("dp", "ctx")),
        P(("dp", "ctx"), None),
        P(None, ("dp", "ctx")),
        P(("dp", "ctx")),
        P(("dp", "ctx")),
        P(("dp", "ctx"), None),
        P(("dp", "ctx"), None),
        P(("dp", "ctx"), None),
        P(("dp", "ctx"), None),
        P(("dp", "ctx")),
        P(("dp", "ctx"), None),
        P(("dp", "ctx"), None),
        P(),
        P(),
        P(),
    )
    return jax.shard_map(
        body,
        mesh=mesh,
        in_specs=placed,
        out_specs=(
            P(None, ("dp", "ctx"), None),
            P(None, ("dp", "ctx"), None),
            P(("dp", "ctx")),
            P(("dp", "ctx"), None),
            P(None, ("dp", "ctx")),
            P(("dp", "ctx")),
            P(("dp", "ctx")),
            P(("dp", "ctx"), None),
            P(("dp", "ctx"), None),
            P(("dp", "ctx"), None),
            P(("dp", "ctx"), None),
            P(("dp", "ctx")),
            P(("dp", "ctx"), None),
            P(("dp", "ctx"), None),
            P(),
            P(),
            P(),
        ),
        check_vma=False,
    )
```

profile of v0, /device:TPU:0, one launch (start us, length us, event | category | flops | bytes accessed | tf_op | source)
XLA Modules:
  0.0 1585.0 jit_solution(13918939086332599000)
XLA Ops:
  45.2 42.2 %all-reduce.42 = (bf16[1024]{0:T(1024)(128)(2,1)S(1)}, bf16[1792]{0:T(1024)(128)(2,1)S(1)}, bf16[1536]{0:T(1024)(128)(2,1)S(1)}, bf16[1024]{0:T(1024)(128)(2,1)S(1)}) all-reduce(bf16[1024]{0:T(1024)(128)(2,1)S(1)} %dynamic-update-slice.1, bf16[1792]{0:T(1024)(128)(2,1)S(1)} %dynamic-update-slice, ...), channel_id=1, replica_groups=mesh['dp'=8,'ctx'=4] {'dp','ctx'}, use_global_device_ids=true, to_apply=%add.33 | all-reduce | flops 5376 | bytes 21504
  87.7 40.8 %all-gather = bf16[32,56,4]{1,2,0:T(4,128)(2,1)S(1)} all-gather(bf16[1,56,4]{1,2,0:T(4,128)(2,1)S(1)} %bitcast.930), channel_id=1, replica_groups=mesh['dp'=8,'ctx'=4] {'dp','ctx'}, dimensions={0}, use_global_device_ids=true | all-gather | bytes 14784 | tf_op jit(solution)/shard_map/all_gather | solution.py:187
  143.3 38.4 %all_gather.34 = bf16[1024,256]{1,0:T(8,128)(2,1)S(1)} all-gather(bf16[32,256]{1,0:T(8,128)(2,1)S(1)} %copy-done.232), channel_id=1, replica_groups=mesh['dp'=8,'ctx'=4] {'dp','ctx'}, dimensions={0}, use_global_device_ids=true | all-gather | bytes 540672 | tf_op jit(solution)/shard_map/all_gather | solution.py:192
  182.1 8.9 all_gather.41
  207.1 9.4 all_gather.35
  291.4 26.0 %while.26 = (s32[]{:T(128)}, bf16[1,24,64,128]{3,2,1,0:T(8,128)(2,1)}, f32[1,24,64,128]{3,2,1,0:T(8,128)}, f32[1,24,1,1]{1,3,2,0:T(1,128)S(1)}, f32[1,24,64,128]{3,2,1,0:T(8,128)S(1)}, /*index=5*/s32[]{:T(128)}) while((s32[]{:T(128)}, bf16[1,24,64,128]{3,2,1,0:T(8,128)(2,1)}, f32[1,24,64,128]{3,2,1,0:T(8,128)}, f32[1,24,1,1]{1,3,2,0:T(1,128)S(1)}, ...), condition=%wide.region_4.6_spmd, body=%wide.region_3.5_spmd.sunk | while | flops 786434 | bytes 3932365 | solution.py:257
  304.5 10.2 collective-permute-start
  322.7 38.0 %while.27 = (s32[]{:T(128)}, bf16[1,24,64,128]{3,2,1,0:T(8,128)(2,1)S(1)}, f32[1,24,64,128]{3,2,1,0:T(8,128)}, f32[1,24,1,1]{1,3,2,0:T(1,128)S(1)}, f32[1,24,64,128]{3,2,1,0:T(8,128)S(1)}, /*index=5*/s32[]{:T(128)}) while((s32[]{:T(128)}, bf16[1,24,64,128]{3,2,1,0:T(8,128)(2,1)S(1)}, f32[1,24,64,128]{3,2,1,0:T(8,128)}, ...), condition=%wide.region_13.15_spmd, body=%wide.region_12.14_spmd.sunk | while | flops 786434 | bytes 3932365 | solution.py:257
  322.7 14.1 collective-permute-start.1
  432.8 47.3 %while.104 = (s32[]{:T(128)}, f32[256,2,4,64]{0,3,2,1:T(8,128)}, bf16[4,256,256]{2,1,0:T(8,128)(2,1)}, s32[4]{0:T(128)S(1)}, bf16[1024,256]{1,0:T(8,128)(2,1)}, ...) while((s32[]{:T(128)}, f32[256,2,4,64]{0,3,2,1:T(8,128)}, ...), condition=%wide.region_32.34_spmd.clone.clone.clone, body=%wide.region_31.33_spmd.clone.clone.clone.sunk | while | flops 340135680 | bytes 15456809 | solution.py:402
  482.7 41.9 %while.105 = (s32[]{:T(128)}, f32[256,2,4,64]{0,3,2,1:T(8,128)}, bf16[4,256,256]{2,1,0:T(8,128)(2,1)}, s32[4]{0:T(128)S(1)}, bf16[1024,256]{1,0:T(8,128)(2,1)}, ...) while((s32[]{:T(128)}, f32[256,2,4,64]{0,3,2,1:T(8,128)}, ...), condition=%wide.region_49.51_spmd.clone.clone.clone, body=%wide.region_48.50_spmd.clone.clone.clone.sunk | while | flops 340135680 | bytes 13359601 | solution.py:402
  527.2 23.6 %reduce-scatter.13.cloned.1.call-done = bf16[256,256]{1,0:T(8,128)(2,1)} async-done(((bf16[1024,256]{1,0:T(8,128)(2,1)}), bf16[256,256]{1,0:T(8,128)(2,1)}) %reduce-scatter.13.cloned.1.call-update) | async-done | bytes 131088 | tf_op jit(solution)/shard_map/reduce_scatter | solution.py:407
  598.6 26.1 %while.28 = (s32[]{:T(128)}, bf16[1,24,64,128]{3,2,1,0:T(8,128)(2,1)}, f32[1,24,64,128]{3,2,1,0:T(8,128)}, f32[1,24,1,1]{1,3,2,0:T(1,128)S(1)}, f32[1,24,64,128]{3,2,1,0:T(8,128)S(1)}, /*index=5*/s32[]{:T(128)}) while((s32[]{:T(128)}, bf16[1,24,64,128]{3,2,1,0:T(8,128)(2,1)}, f32[1,24,64,128]{3,2,1,0:T(8,128)}, ...), condition=%wide.region_22.24_spmd, body=%wide.region_21.23_spmd.sunk | while | flops 786434 | bytes 3932365 | solution.py:423
  630.0 32.4 %while.29 = (s32[]{:T(128)}, bf16[1,24,64,128]{3,2,1,0:T(8,128)(2,1)S(1)}, f32[1,24,64,128]{3,2,1,0:T(8,128)}, f32[1,24,1,1]{1,3,2,0:T(1,128)S(1)}, f32[1,24,64,128]{3,2,1,0:T(8,128)S(1)}, /*index=5*/s32[]{:T(128)}) while((s32[]{:T(128)}, bf16[1,24,64,128]{3,2,1,0:T(8,128)(2,1)S(1)}, f32[1,24,64,128]{3,2,1,0:T(8,128)}, ...), condition=%wide.region_39.41_spmd, body=%wide.region_38.40_spmd.sunk | while | flops 786434 | bytes 3932365 | solution.py:423
  682.4 9.7 fusion.195
  704.2 11.4 fusion.193
  771.1 11.0 fusion.290
  782.1 14.1 convolution_add_fusion.1
  823.7 49.3 %all-reduce.41 = (f32[1024]{0:T(1024)S(1)}, f32[4,1792]{1,0:T(4,128)S(1)}, f32[1792]{0:T(1024)S(1)}, f32[1536]{0:T(1024)S(1)}, f32[1024]{0:T(1024)S(1)}, /*index=5*/f32[24]{0:T(128)}, f32[24]{0:T(128)}, f32[24]{0:T(128)}) all-reduce(f32[1024]{0:T(1024)S(1)} %add.763, ...), channel_id=4, replica_groups=mesh['dp'=8,'ctx'=4] {'dp','ctx'}, use_global_device_ids=true, to_apply=%region_54.56.clone | all-reduce | flops 12616 | bytes 100928
  879.5 80.4 %reduce-scatter.23.cloned.1.call-done = f32[16,1024]{1,0:T(8,128)} async-done(((f32[512,1024]{1,0:T(8,128)}), f32[16,1024]{1,0:T(8,128)}) %reduce-scatter.23.cloned.1.call-update) | async-done | bytes 65552 | tf_op jit(solution)/shard_map/reduce_scatter | solution.py:466
  959.9 117.5 %reduce-scatter.17.cloned.1.call-done = f32[48,1024]{1,0:T(8,128)} async-done(((f32[1536,1024]{1,0:T(8,128)}), f32[48,1024]{1,0:T(8,128)}) %reduce-scatter.17.cloned.1.call-update) | async-done | bytes 196624 | tf_op jit(solution)/shard_map/reduce_scatter | solution.py:463
  1077.4 151.1 %reduce-scatter.27.cloned.1.call-done = f32[64,1024]{1,0:T(8,128)} async-done(((f32[2048,1024]{1,0:T(8,128)}), f32[64,1024]{1,0:T(8,128)}) %reduce-scatter.27.cloned.1.call-update) | async-done | bytes 262160 | tf_op jit(solution)/shard_map/reduce_scatter | solution.py:469
  1228.5 165.2 %reduce-scatter.15.cloned.1.call-done = f32[32,3352]{1,0:T(8,128)} async-done(((f32[1024,3352]{1,0:T(8,128)}), f32[32,3352]{1,0:T(8,128)}) %reduce-scatter.15.cloned.1.call-update) | async-done | bytes 429072 | tf_op jit(solution)/shard_map/reduce_scatter | solution.py:459
  1393.7 184.5 %reduce-scatter.25.cloned.1.call-done = f32[32,4096]{1,0:T(8,128)} async-done(((f32[1024,4096]{1,0:T(8,128)}), f32[32,4096]{1,0:T(8,128)}) %reduce-scatter.25.cloned.1.call-update) | async-done | bytes 524304 | tf_op jit(solution)/shard_map/reduce_scatter | solution.py:468
  (1251 shorter events, 572.9 us)
Async XLA Ops:
  7.2 211.1 %all-gather.12.cloned.1.call-start = ((), (), s32[]{:S(2)}) async-start(), calls=%async_computation.11 | async-start | bytes 1081344 | tf_op jit(solution)/shard_map/all_gather | solution.py:191
  7.9 230.6 %all-gather.8.cloned.1.call-start = ((), (), s32[]{:S(2)}) async-start(), calls=%async_computation.9 | async-start | bytes 7299072 | tf_op jit(solution)/shard_map/all_gather | solution.py:186
  8.7 374.6 %all-gather.10.cloned.1.call-start = ((), (), s32[]{:S(2)}) async-start(), calls=%async_computation.10 | async-start | bytes 3244032 | tf_op jit(solution)/shard_map/all_gather | solution.py:190
  9.4 378.9 %all-gather.14.cloned.1.call-start = ((), (), s32[]{:S(2)}) async-start(), calls=%async_computation.12 | async-start | bytes 1081344 | tf_op jit(solution)/shard_map/all_gather | solution.py:193
  10.0 383.4 %all-gather.16.cloned.1.call-start = ((), (), s32[]{:S(2)}) async-start(), calls=%async_computation.13 | async-start | bytes 8650752 | tf_op jit(solution)/shard_map/all_gather | solution.py:195
  10.6 395.7 %all-gather.18.cloned.1.call-start = ((), (), s32[]{:S(2)}) async-start(), calls=%async_computation.14 | async-start | bytes 4325376 | tf_op jit(solution)/shard_map/all_gather | solution.py:196
  11.1 513.5 %reduce-scatter.11.cloned.1.call-start = ((), (), s32[]{:S(2)}) async-start(), calls=%async_computation.15 | async-start | bytes 655360 | tf_op jit(solution)/shard_map/reduce_scatter | solution.py:407
  254.6 11.9 collective-permute-start.4
  304.5 11.7 collective-permute-start
  322.7 15.5 collective-permute-start.1
  349.2 10.0 collective-permute-start.1
  480.1 70.7 %reduce-scatter.13.cloned.1.call-start = ((), (), s32[]{:S(2)}) async-start(), calls=%async_computation.16 | async-start | bytes 655360 | tf_op jit(solution)/shard_map/reduce_scatter | solution.py:407
  524.6 354.9 %reduce-scatter.21.cloned.1.call-start = ((), (), s32[]{:S(2)}) async-start(), calls=%async_computation.20 | async-start | bytes 1081344 | tf_op jit(solution)/shard_map/reduce_scatter | solution.py:465
  553.6 325.9 %reduce-scatter.19.cloned.1.call-start = ((), (), s32[]{:S(2)}) async-start(), calls=%async_computation.19 | async-start | bytes 2162688 | tf_op jit(solution)/shard_map/reduce_scatter | solution.py:464
  556.8 403.1 %reduce-scatter.23.cloned.1.call-start = ((), (), s32[]{:S(2)}) async-start(), calls=%async_computation.21 | async-start | bytes 2162688 | tf_op jit(solution)/shard_map/reduce_scatter | solution.py:466
  560.2 517.2 %reduce-scatter.17.cloned.1.call-start = ((), (), s32[]{:S(2)}) async-start(), calls=%async_computation.18 | async-start | bytes 6488064 | tf_op jit(solution)/shard_map/reduce_scatter | solution.py:463
  567.4 661.1 %reduce-scatter.27.cloned.1.call-start = ((), (), s32[]{:S(2)}) async-start(), calls=%async_computation.23 | async-start | bytes 8650752 | tf_op jit(solution)/shard_map/reduce_scatter | solution.py:469
  630.0 9.7 collective-permute-start.3
  640.7 9.7 collective-permute-start.3
  651.5 9.8 collective-permute-start.3
  673.6 720.0 %reduce-scatter.15.cloned.1.call-start = ((), (), s32[]{:S(2)}) async-start(), calls=%async_computation.17 | async-start | bytes 14598144 | tf_op jit(solution)/shard_map/reduce_scatter | solution.py:459
  744.3 13.1 collective-permute-start.7
  749.0 10.0 collective-permute-start.6
  770.5 807.7 %reduce-scatter.25.cloned.1.call-start = ((), (), s32[]{:S(2)}) async-start(), calls=%async_computation.22 | async-start | bytes 17301504 | tf_op jit(solution)/shard_map/reduce_scatter | solution.py:468
  (381 other events, 6229.6 us)
Sparse Core Ops, SparseCore 0:
  10.9 56.4 all-gather.11
  70.3 72.1 all-gather.7
  145.4 57.5 all-gather.9
  205.7 52.5 all-gather.13
  261.0 76.5 all-gather.15
  340.3 64.7 all-gather.17
  480.2 26.0 reduce-scatter.10
  524.7 26.0 reduce-scatter.12
  553.7 134.9 reduce-scatter.20
  691.5 132.9 reduce-scatter.18
  827.3 132.5 reduce-scatter.22
  966.9 110.4 reduce-scatter.16
  1080.2 148.2 reduce-scatter.26
  1234.9 158.6 reduce-scatter.14
  1396.4 181.7 reduce-scatter.24
where the time goes:
time: 1600 us; the launch traced here: 1580 us
  waiting for transfers between devices  779 us (49%)
  matrix products  323 us (20%)
  blocking collectives  189 us (12%)
  local copies, waits for them, and re-layouts  110 us (7%)
  other arithmetic  88.2 us (6%)
  starting transfers between devices  65.8 us (4%)
  between operations  23.7 us (1%)
    reduce_scatter x1, waiting for transfers between devices, body(): lax.psum_scatter(totals[10], ('dp', 'ctx'), scatter_dimension=0, tiled=True)  185 us
    reduce_scatter x1, waiting for transfers between devices, body(): lax.psum_scatter(totals[1], ('dp', 'ctx'), scatter_dimension=0, tiled=True)  165 us
    reduce_scatter x1, waiting for transfers between devices, body(): lax.psum_scatter(totals[11], ('dp', 'ctx'), scatter_dimension=0, tiled=True)  151 us
    reduce_scatter x1, waiting for transfers between devices, body(): lax.psum_scatter(totals[5], ('dp', 'ctx'), scatter_dimension=0, tiled=True)  117 us
    unnamed x2, blocking collectives  91.4 us
    reduce_scatter x1, waiting for transfers between devices, body(): lax.psum_scatter(totals[8], ('dp', 'ctx'), scatter_dimension=0, tiled=True)  80.4 us
    ppermute x16, starting transfers between devices, from_behind(): return lax.ppermute(block, axis, route)  64.8 us
    dot_general x14, matrix products, left_dot(): lax.dot_general(first_arg, second_arg, (((0,), (0,)), ((), ())), preferre...  56.6 us
  transfers between devices with their start and end apart: 31, of which 18 were waited for; matrix products, arithmetic and copies ran while one was open for 27% of the time, Pallas kernels for 0%

commit v1 on v0

v1 whole, which is shorter than its diff:
```python
import functools

import jax
import jax.numpy as jnp
from jax import lax
from jax.sharding import PartitionSpec as P

MH = 24
HP = 64
NS = 128
CONV = 4
AH = 8
KVH = 2
AD = 64
DI = 1536
XC = 1792
QD = 512
KD = 128


EPSILON = 1e-05
HIGHEST = lax.Precision.HIGHEST
MASKED = -1e30
EVERY = ("dp", "ctx")


def bit_list(count):
    bits = []
    size = 1
    while size < count:
        bits.append(size)
        size *= 2
    return bits


def swap_with(block, axes, count, bit):
    return lax.ppermute(block, axes, [(i, i ^ bit) for i in range(count)])


def spread(shard, axes, count, order):
    me = lax.axis_index(axes)
    held = shard[None]
    for bit in order:
        other = swap_with(held, axes, count, bit)
        upper = ((me // bit) % 2) == 1
        held = jnp.stack([jnp.where(upper, other, held), jnp.where(upper, held, other)])
    places = len(order)
    held = held.reshape((2,) * places + shard.shape)
    dims = order[::-1]
    turned = sorted(range(places), key=lambda k: -dims[k])
    held = held.transpose(tuple(turned) + tuple(range(places, places + shard.ndim)))
    return held.reshape((count,) + shard.shape)


def collect(parts, axes, count, order):
    me = lax.axis_index(axes)
    left = sorted(order, reverse=True)
    held = parts.reshape((2,) * len(order) + parts.shape[1:])
    for bit in order:
        at = left.index(bit)
        left.pop(at)
        upper = (me // bit) % 2
        kept = lax.dynamic_index_in_dim(held, upper, at, keepdims=False)
        sent = lax.dynamic_index_in_dim(held, 1 - upper, at, keepdims=False)
        other = swap_with(sent, axes, count, bit)
        held = (kept.astype(jnp.float32) + other.astype(jnp.float32)).astype(parts.dtype)
    return held


def sum_all(value, axes, count):
    for bit in bit_list(count):
        value = value + swap_with(value, axes, count, bit)
    return value


def chain_states(state, decay, axis, count, backward):
    me = lax.axis_index(axis)
    prefix = jnp.zeros_like(state)
    prefix_decay = jnp.ones_like(decay)
    total, total_decay = state, decay
    for bit in bit_list(count):
        other = swap_with(total.astype(jnp.bfloat16), axis, count, bit).astype(jnp.float32)
        other_decay = swap_with(total_decay, axis, count, bit)
        upper = ((me // bit) % 2) == 1
        later = jnp.logical_not(upper) if backward else upper
        prefix = jnp.where(later, prefix + prefix_decay * other, prefix)
        prefix_decay = jnp.where(later, prefix_decay * other_decay, prefix_decay)
        total = jnp.where(later, total + total_decay * other, other + other_decay * total)
        total_decay = total_decay * other_decay
    return prefix


def rms_scale(signal, scale):
    return signal * lax.rsqrt(jnp.mean(signal * signal, axis=-1, keepdims=True) + EPSILON) * scale


def swiglu(joined):
    half_cols = joined.shape[1] // 2
    return jax.nn.silu(joined[:, :half_cols]) * joined[:, half_cols:]


def plain_dot(first_arg, second_arg):
    return jnp.dot(first_arg, second_arg, preferred_element_type=jnp.float32)


def left_dot(first_arg, second_arg):
    return lax.dot_general(
        first_arg, second_arg, (((0,), (0,)), ((), ())), preferred_element_type=jnp.float32
    )


def right_dot(first_arg, second_arg):
    return lax.dot_general(
        first_arg, second_arg, (((1,), (1,)), ((), ())), preferred_element_type=jnp.float32
    )


def by_head(array):
    micro, rows, _ = array.shape
    return array.reshape(micro, rows, MH, HP).transpose(0, 2, 1, 3)


def mamba_local(xbc, raw_step, tail, w_conv, b_conv, log_a, bias_dt, skip_val, alive, allowed, offset):
    rows = xbc.shape[1]
    reach = CONV - 1
    longer = jnp.concatenate([tail, xbc], axis=1)
    convolved = b_conv + w_conv[reach] * xbc
    for shift_by in range(1, CONV):
        shifted = longer[:, reach - shift_by : reach - shift_by + rows]
        inside = alive | (offset >= shift_by)
        convolved = convolved + jnp.where(inside[..., None], shifted, 0.0) * w_conv[reach - shift_by]
    activated = jax.nn.silu(convolved)
    values = by_head(activated[..., :DI])
    b_in = activated[..., DI : DI + NS]
    c_out = activated[..., DI + NS :]
    step_size = jax.nn.softplus(raw_step + bias_dt).transpose(0, 2, 1)
    log_decay = -step_size * jnp.exp(log_a)[:, None]
    scaled = values * step_size[..., None]
    before = jnp.triu(jnp.ones((rows, rows), jnp.float32))
    within = jnp.einsum("mhs,st->mht", log_decay, before, precision=HIGHEST)
    live = alive.astype(jnp.float32)[:, None, :]
    span_sum = jnp.sum(log_decay * live, axis=-1, keepdims=True)
    inner_cb = jnp.einsum("mtn,msn->mts", c_out, b_in)
    gap = jnp.minimum(within[..., :, None] - within[..., None, :], 0.0)
    mixing = jnp.where(allowed[:, None], jnp.exp(gap), 0.0) * inner_cb[:, None]
    local_out = jnp.einsum("mhts,mhsp->mhtp", mixing, scaled) + skip_val[:, None, None] * values
    to_end = jnp.exp(jnp.minimum(span_sum - within, 0.0)) * live
    end_state = jnp.einsum("mhsp,msn->mhpn", scaled * to_end[..., None], b_in)
    from_start = jnp.exp(within) * live
    return (local_out, end_state, jnp.exp(span_sum), c_out, from_start)


def mamba_finish(local_out, c_out, from_start, state_in, gate_input, gate_scale):
    carried = jnp.einsum("mtn,mhpn->mhtp", c_out, state_in) * from_start[..., None]
    full_out = (local_out + carried).transpose(0, 2, 1, 3).reshape(gate_input.shape)
    return rms_scale(full_out * jax.nn.silu(gate_input), gate_scale)


def body(
    dp_count,
    ctx_count,
    hidden,
    cotangent,
    seq_lengths,
    norm_gain,
    in_proj,
    conv_weight,
    conv_bias,
    gate_gain,
    out_proj,
    q_proj,
    kv_proj,
    o_proj,
    ff_gain,
    gate_up,
    down_proj,
    a_log,
    dt_bias,
    skip_scale,
):
    count = dp_count * ctx_count
    ctx_place = lax.axis_index("ctx")
    micro, rows, width = hidden.shape
    all_rows = micro * rows
    groups = AH // KVH
    scale_qk = AD ** (-0.5)
    bits = bit_list(count)
    order_a = bits[::-1]
    order_b = list(order_a)
    if count == 32:
        order_a = [16, 8, 4, 2, 1]
        order_b = [16, 8, 2, 4, 1]

    small_parts = (norm_gain, conv_weight.reshape(-1), conv_bias, gate_gain, ff_gain)
    small_sizes = [part.shape[0] for part in small_parts]
    small_width = -(-sum(small_sizes) // 128) * 128
    pad = small_width - sum(small_sizes)
    small_shard = jnp.concatenate(small_parts + (jnp.zeros((pad,), jnp.bfloat16),))
    small_all = spread(small_shard.reshape(-1, 128), EVERY, count, order_a).reshape(count, -1)
    cut = [0]
    for size in small_sizes:
        cut.append(cut[-1] + size)
    g_norm = small_all[:, cut[0] : cut[1]].reshape(-1).astype(jnp.float32)
    w_conv = (
        small_all[:, cut[1] : cut[2]]
        .reshape(count, CONV, -1)
        .transpose(1, 0, 2)
        .reshape(CONV, -1)
        .astype(jnp.float32)
    )
    b_conv = small_all[:, cut[2] : cut[3]].reshape(-1).astype(jnp.float32)
    g_gate = small_all[:, cut[3] : cut[4]].reshape(-1).astype(jnp.float32)
    g_ff = small_all[:, cut[4] : cut[5]].reshape(-1).astype(jnp.float32)

    front_shard = jnp.concatenate([q_proj, kv_proj, in_proj], axis=1)
    halfway = front_shard.shape[0] // 2
    front_low = spread(front_shard[:halfway], EVERY, count, order_a)
    front_high = spread(front_shard[halfway:], EVERY, count, order_b)
    w_front = jnp.concatenate([front_low, front_high], axis=1).reshape(width, -1)
    close_shard = jnp.concatenate([out_proj, o_proj], axis=0)
    close_all = spread(close_shard, EVERY, count, order_b)
    out_rows = out_proj.shape[0]
    w_out = close_all[:, :out_rows].reshape(-1, width)
    w_o = close_all[:, out_rows:].reshape(-1, width)
    w_gu = spread(gate_up, EVERY, count, order_a).reshape(width, -1)
    w_down = spread(down_proj, EVERY, count, order_b).reshape(-1, width)

    span_len = seq_lengths[0, :, 0] // ctx_count
    local_row = jnp.arange(rows, dtype=jnp.int32)[None, :]
    alive = local_row < span_len[:, None]
    offset = jnp.where(alive, local_row, local_row - span_len[:, None])
    extent = jnp.where(alive, span_len[:, None], rows - span_len[:, None])
    position = ctx_place * extent + offset
    same = alive[:, :, None] == alive[:, None, :]
    causal = local_row[0][:, None] >= local_row[0][None, :]
    alive_row = alive.reshape(-1, 1).astype(jnp.float32)

    x_in = hidden.reshape(all_rows, width).astype(jnp.float32)
    normed, norm_pull = jax.vjp(rms_scale, x_in, g_norm)
    normed_b = normed.astype(jnp.bfloat16)
    joined = plain_dot(normed_b, w_front).astype(jnp.bfloat16)
    query_b = joined[:, :QD]
    keyval_b = joined[:, QD : QD + 2 * KD]
    mixed = joined[:, QD + 2 * KD :]
    gate_z = mixed[:, :DI].astype(jnp.float32).reshape(micro, rows, DI)
    xbc_b = mixed[:, DI : DI + XC].reshape(micro, rows, XC)
    raw_step = mixed[:, DI + XC :].astype(jnp.float32).reshape(micro, rows, MH)

    reach = CONV - 1
    tail_rows = jnp.stack(
        [
            lax.dynamic_slice_in_dim(xbc_b[index], span_len[index] - reach, reach, 0)
            for index in range(micro)
        ]
    )
    tail_in = lax.ppermute(tail_rows, "ctx", [(i, i + 1) for i in range(ctx_count - 1)])
    ctx_order = bit_list(ctx_count)[::-1]
    every_kv = spread(keyval_b.reshape(micro, rows, 2 * KD), "ctx", ctx_count, ctx_order)

    def mamba_front(*args):
        return mamba_local(*args, alive, same & causal, offset)

    front_out, front_pull = jax.vjp(
        mamba_front,
        xbc_b.astype(jnp.float32),
        raw_step,
        tail_in.astype(jnp.float32),
        w_conv,
        b_conv,
        a_log,
        dt_bias,
        skip_scale,
    )
    local_out, end_state, span_decay, c_out, from_start = front_out
    decay_wide = span_decay[..., None]
    state_in = chain_states(end_state, decay_wide, "ctx", ctx_count, False)

    query_heads = query_b.reshape(micro, rows, KVH, groups, AD).transpose(0, 2, 3, 1, 4)
    key_heads = every_kv[..., :KD].reshape(ctx_count, micro, rows, KVH, AD).transpose(1, 3, 0, 2, 4)
    key_heads = key_heads.reshape(micro, KVH, ctx_count * rows, AD)
    value_heads = every_kv[..., KD:].reshape(ctx_count, micro, rows, KVH, AD)
    value_heads = value_heads.transpose(1, 3, 0, 2, 4).reshape(micro, KVH, ctx_count * rows, AD)
    source = jnp.arange(ctx_count, dtype=jnp.int32)[None, :, None]
    key_pos = (source * extent[:, None, :] + offset[:, None, :]).reshape(micro, -1)
    key_alive = jnp.broadcast_to(alive[:, None, :], (micro, ctx_count, rows)).reshape(micro, -1)
    seen = (alive[:, :, None] == key_alive[:, None, :]) & (
        position[:, :, None] >= key_pos[:, None, :]
    )
    seen = seen[:, None, None]
    scores = (
        jnp.einsum("mgjtd,mgsd->mgjts", query_heads, key_heads, preferred_element_type=jnp.float32)
        * scale_qk
    )
    scores = jnp.where(seen, scores, MASKED)
    weights = jnp.exp(scores - jnp.max(scores, axis=-1, keepdims=True))
    probs = weights / jnp.sum(weights, axis=-1, keepdims=True)
    probs_b = probs.astype(jnp.bfloat16)
    attended = jnp.einsum(
        "mgjts,mgsd->mgjtd", probs_b, value_heads, preferred_element_type=jnp.float32
    )
    attended_b = attended.transpose(0, 3, 1, 2, 4).reshape(all_rows, QD).astype(jnp.bfloat16)
    attn_branch = plain_dot(attended_b, w_o)

    mamba_norm, finish_pull = jax.vjp(
        mamba_finish, local_out, c_out, from_start, state_in, gate_z, g_gate
    )
    mamba_norm_b = mamba_norm.reshape(all_rows, DI).astype(jnp.bfloat16)
    middle = x_in + plain_dot(mamba_norm_b, w_out) + attn_branch
    normed_ff, ff_pull = jax.vjp(rms_scale, middle, g_ff)
    normed_ff_b = normed_ff.astype(jnp.bfloat16)
    gate_up_b = plain_dot(normed_ff_b, w_gu).astype(jnp.bfloat16)
    activation, act_pull = jax.vjp(swiglu, gate_up_b.astype(jnp.float32))
    activation_b = activation.astype(jnp.bfloat16)
    layer_out = ((middle + plain_dot(activation_b, w_down)) * alive_row).astype(jnp.bfloat16)

    def owned(grad, order):
        return collect(grad.reshape((count, -1) + grad.shape[1:]), EVERY, count, order)

    back_a = order_a[::-1]
    back_b = order_b[::-1]
    d_out = cotangent.reshape(all_rows, width).astype(jnp.float32) * alive_row
    d_ff_b = d_out.astype(jnp.bfloat16)
    r_down = owned(left_dot(activation_b, d_ff_b).astype(jnp.bfloat16), back_b)
    (d_gate_up,) = act_pull(right_dot(d_ff_b, w_down))
    d_gate_up_b = d_gate_up.astype(jnp.bfloat16)
    r_gu = owned(left_dot(normed_ff_b, d_gate_up_b).astype(jnp.bfloat16), back_a)
    d_mid_part, g_ffgain = ff_pull(right_dot(d_gate_up_b, w_gu))
    d_mid = d_out + d_mid_part
    d_branch_b = d_mid.astype(jnp.bfloat16)
    d_mamba_norm = right_dot(d_branch_b, w_out).reshape(micro, rows, DI)
    d_local, d_cout, d_from, d_state_in, d_gate_z, g_gategain = finish_pull(d_mamba_norm)
    d_end_state = chain_states(d_state_in, decay_wide, "ctx", ctx_count, True)
    g_close = jnp.concatenate(
        [
            left_dot(mamba_norm_b, d_branch_b).astype(jnp.bfloat16).reshape(count, -1, width),
            left_dot(attended_b, d_branch_b).astype(jnp.bfloat16).reshape(count, -1, width),
        ],
        axis=1,
    )
    r_close = collect(g_close, EVERY, count, back_b)

    d_attended_b = right_dot(d_branch_b, w_o).astype(jnp.bfloat16)
    d_att_heads = d_attended_b.reshape(micro, rows, KVH, groups, AD).transpose(0, 2, 3, 1, 4)
    d_probs = jnp.einsum(
        "mgjtd,mgsd->mgjts", d_att_heads, value_heads, preferred_element_type=jnp.float32
    )
    row_delta = jnp.sum(d_att_heads.astype(jnp.float32) * attended, axis=-1, keepdims=True)
    d_score = (probs * (d_probs - row_delta)).astype(jnp.bfloat16)
    d_query = jnp.einsum(
        "mgjts,mgsd->mtgjd", d_score, key_heads, preferred_element_type=jnp.float32
    )
    d_query_b = (d_query * scale_qk).reshape(all_rows, QD).astype(jnp.bfloat16)
    d_keys = jnp.einsum(
        "mgjts,mgjtd->msgd", d_score, query_heads, preferred_element_type=jnp.float32
    )
    d_values = jnp.einsum(
        "mgjts,mgjtd->msgd", probs_b, d_att_heads, preferred_element_type=jnp.float32
    )
    d_kv_parts = jnp.concatenate(
        [
            (d_keys * scale_qk).reshape(micro, ctx_count, rows, KD),
            d_values.reshape(micro, ctx_count, rows, KD),
        ],
        axis=-1,
    ).transpose(1, 0, 2, 3)
    d_keyval = collect(d_kv_parts.astype(jnp.bfloat16), "ctx", ctx_count, ctx_order[::-1])
    d_keyval = d_keyval.reshape(all_rows, 2 * KD)

    d_span_decay = jnp.sum(d_end_state * state_in, axis=(2, 3))[..., None]
    d_xbc, d_raw_step, d_tail, g_conv, g_convbias, g_alog, g_dtbias, g_skip = front_pull(
        (d_local, d_end_state, d_span_decay, d_cout, d_from)
    )
    tail_back = lax.ppermute(d_tail, "ctx", [(i + 1, i) for i in range(ctx_count - 1)])
    row_index = jnp.arange(rows, dtype=jnp.int32)[None, :]
    for step in range(reach):
        hit = row_index == (span_len[:, None] - reach + step)
        d_xbc = d_xbc + jnp.where(hit[..., None], tail_back[:, step : step + 1], 0.0)
    d_joined_b = jnp.concatenate(
        [
            d_query_b,
            d_keyval,
            d_gate_z.reshape(all_rows, DI).astype(jnp.bfloat16),
            d_xbc.reshape(all_rows, XC).astype(jnp.bfloat16),
            d_raw_step.reshape(all_rows, MH).astype(jnp.bfloat16),
        ],
        axis=1,
    )
    g_front = left_dot(normed_b, d_joined_b).astype(jnp.bfloat16)
    g_front = g_front.reshape((count, 2, halfway, -1))
    r_front = jnp.concatenate(
        [collect(g_front[:, 0], EVERY, count, back_a), collect(g_front[:, 1], EVERY, count, back_b)],
        axis=0,
    ).astype(jnp.float32)
    d_x_part, g_normgain = norm_pull(right_dot(d_joined_b, w_front))
    grad_hidden = (d_mid + d_x_part).astype(jnp.bfloat16)

    small_grads = jnp.concatenate(
        [
            g_normgain.reshape(count, -1),
            g_conv.reshape(CONV, count, -1).transpose(1, 0, 2).reshape(count, -1),
            g_convbias.reshape(count, -1),
            g_gategain.reshape(count, -1),
            g_ffgain.reshape(count, -1),
            jnp.zeros((count, pad), jnp.float32),
        ],
        axis=1,
    ).reshape(count, -1, 128)
    r_small = collect(small_grads, EVERY, count, back_a).reshape(-1)
    heads = jnp.concatenate([g_alog, g_dtbias, g_skip, jnp.zeros((128 - 3 * MH,), jnp.float32)])
    heads = sum_all(heads.reshape(1, 128), EVERY, count)[0]
    own = [r_small[cut[k] : cut[k + 1]] for k in range(5)]
    r_close = r_close.astype(jnp.float32)
    return (
        layer_out.reshape(hidden.shape),
        grad_hidden.reshape(hidden.shape),
        own[0],
        r_front[:, QD + 2 * KD :],
        own[1].reshape(CONV, -1),
        own[2],
        own[3],
        r_close[:out_rows],
        r_front[:, :QD],
        r_front[:, QD : QD + 2 * KD],
        r_close[out_rows:],
        own[4],
        r_gu.astype(jnp.float32),
        r_down.astype(jnp.float32),
        heads[:MH],
        heads[MH : 2 * MH],
        heads[2 * MH : 3 * MH],
    )


def solution(mesh):
    placed = (
        P(None, ("dp", "ctx"), None),
        P(None, ("dp", "ctx"), None),
        P("dp", None, None),
        P(("dp", "ctx")),
        P(("dp", "ctx"), None),
        P(None, ("dp", "ctx")),
        P(("dp", "ctx")),
        P(("dp", "ctx")),
        P(("dp", "ctx"), None),
        P(("dp", "ctx"), None),
        P(("dp", "ctx"), None),
        P(("dp", "ctx"), None),
        P(("dp", "ctx")),
        P(("dp", "ctx"), None),
        P(("dp", "ctx"), None),
        P(),
        P(),
        P(),
    )
    return jax.shard_map(
        functools.partial(body, mesh.shape["dp"], mesh.shape["ctx"]),
        mesh=mesh,
        in_specs=placed,
        out_specs=(
            P(None, ("dp", "ctx"), None),
            P(None, ("dp", "ctx"), None),
            P(("dp", "ctx")),
            P(("dp", "ctx"), None),
            P(None, ("dp", "ctx")),
            P(("dp", "ctx")),
            P(("dp", "ctx")),
            P(("dp", "ctx"), None),
            P(("dp", "ctx"), None),
            P(("dp", "ctx"), None),
            P(("dp", "ctx"), None),
            P(("dp", "ctx")),
            P(("dp", "ctx"), None),
            P(("dp", "ctx"), None),
            P(),
            P(),
            P(),
        ),
        check_vma=False,
    )
```

time: 1600 us -> 849 us (0.53)
  waiting for transfers between devices: 779 us -> 291 us
  blocking collectives: 189 us -> 0 us
  matrix products: 323 us -> 164 us
  other arithmetic: 88.2 us -> 137 us
  local copies, waits for them, and re-layouts: 110 us -> 153 us
  starting transfers between devices: 65.8 us -> 86.2 us
  between operations: 23.7 us -> 6.73 us
    reduce_scatter x9 -> x0, waiting for transfers between devices: 722 us -> none  [the longest x1 185 us: body(): lax.psum_scatter(totals[10], ('dp', 'ctx'), scatter_dimension=0, tiled=True)]
    ppermute x16 -> x76, waiting for transfers between devices: 52.6 us -> 291 us  [the longest x74 291 us: swap_with(): return lax.ppermute(block, axes, [(i, i ^ bit) for i in range(count)])]
    dot_general x100 -> x19, matrix products: 189 us -> 70.1 us  [the longest x3 21.6 us: mamba_local(): jnp.einsum('mhts,mhsp->mhtp', mixing, scaled)]
    all_gather x4 -> x0, blocking collectives: 97.5 us -> none  [the longest x1 40.8 us: body(): lax.all_gather(conv_weight, ('dp', 'ctx'), axis=1, tiled=True)]
    unnamed x2 -> x0, blocking collectives: 91.4 us -> none
    convert_element_type x21 -> x45, other arithmetic: 4.4 us -> 55.3 us  [the longest x24 22.1 us: collect(): (kept.astype(jnp.float32) + other.astype(jnp.float32)).astype(parts.dtype)]
    gather x6 -> x0, local copies, waits for them, and re-layouts: 41 us -> none  [the longest x4 27.3 us: body(): key_pos = source * extent[local_key] + offset[local_key]]
    dot_general x14 -> x5, matrix products: 56.6 us -> 26.5 us  [left_dot(): lax.dot_general(first_arg, second_arg, (((0,), (0,)), ((), ())), preferre...]
  transfers between devices with their start and end apart: 31 -> 76, of which waited for: 18 -> 38; matrix products, arithmetic and copies ran while one was open for 27% -> 41% of each run, Pallas kernels for 0% -> 0%
where the time goes in v1:
time: 849 us; the launch traced here: 838 us
  waiting for transfers between devices  291 us (34%)
  matrix products  164 us (19%)
  local copies, waits for them, and re-layouts  153 us (18%)
  other arithmetic  137 us (16%)
  starting transfers between devices  86.2 us (10%)
    ppermute x74, waiting for transfers between devices, swap_with(): return lax.ppermute(block, axes, [(i, i ^ bit) for i in range(count)])  291 us
    ppermute x74, starting transfers between devices, swap_with(): return lax.ppermute(block, axes, [(i, i ^ bit) for i in range(count)])  82.4 us
    dot_general x5, matrix products, right_dot(): lax.dot_general(first_arg, second_arg, (((1,), (1,)), ((), ())), preferre...  33.6 us
    dot_general x5, matrix products, left_dot(): lax.dot_general(first_arg, second_arg, (((0,), (0,)), ((), ())), preferre...  26.5 us
    another operation x69, other arithmetic, spread(): jnp.stack([jnp.where(upper, other, held), jnp.where(upper, held, other)])  26 us
    dot_general x5, matrix products, plain_dot(): return jnp.dot(first_arg, second_arg, preferred_element_type=jnp.float32)  23.8 us
    unnamed x318, local copies, waits for them, and re-layouts  22.8 us
    convert_element_type x24, other arithmetic, collect(): (kept.astype(jnp.float32) + other.astype(jnp.float32)).astype(parts.dtype)  22.1 us
  transfers between devices with their start and end apart: 76, of which 38 were waited for; matrix products, arithmetic and copies ran while one was open for 41% of the time, Pallas kernels for 0%

profile of v1, /device:TPU:0, one launch (start us, length us, event | category | flops | bytes accessed | tf_op | source)
XLA Modules:
  0.0 838.3 jit_solution(6118832509736132319)
XLA Ops:
  23.9 10.4 %collective-permute-done = bf16[1,4,128]{2,1,0:T(4,128)(2,1)S(1)} collective-permute-done((bf16[1,4,128]{2,1,0:T(4,128)(2,1)S(1)}, bf16[1,4,128]{2,1,0:T(4,128)(2,1)S(1)}, u32[]{:S(2)}, u32[]{:S(2)}) %collective-permute-start) | collective-permute-done | bytes 1056 | tf_op jit(solution)/shard_map/ppermute | solution.py:37
  87.7 9.1 %collective-permute-done.27 = bf16[2,1,32,4096]{3,2,0,1:T(8,128)(2,1)S(1)} collective-permute-done((bf16[2,1,32,4096]{3,2,0,1:T(8,128)(2,1)S(1)}, bf16[2,1,32,4096]{3,2,0,1:T(8,128)(2,1)S(1)}, u32[]{:S(2)}, u32[]{:S(2)}) %collective-permute-start.27) | collective-permute-done | bytes 524320 | tf_op jit(solution)/shard_map/ppermute | solution.py:37
  108.5 14.6 %collective-permute-done.28 = bf16[2,2,1,32,4096]{4,3,0,1,2:T(8,128)(2,1)S(1)} collective-permute-done((bf16[2,2,1,32,4096]{4,3,0,1,2:T(8,128)(2,1)S(1)}, bf16[2,2,1,32,4096]{4,3,0,1,2:T(8,128)(2,1)S(1)}, u32[]{:S(2)}, u32[]{:S(2)}) %collective-permute-start.28) | collective-permute-done | bytes 1048608 | tf_op jit(solution)/shard_map/ppermute | solution.py:37
  125.1 20.5 %collective-permute-done.34 = bf16[2,2,2,1,64,1024]{5,4,2,1,0,3:T(8,128)(2,1)S(1)} collective-permute-done((bf16[2,2,2,1,64,1024]{5,4,2,1,0,3:T(8,128)(2,1)S(1)}, bf16[2,2,2,1,64,1024]{5,4,2,1,0,3:T(8,128)(2,1)S(1)}, u32[]{:S(2)}, u32[]{:S(2)}) %collective-permute-start.34) | collective-permute-done | bytes 1048608 | tf_op jit(solution)/shard_map/ppermute | solution.py:37
  146.2 21.9 %collective-permute-done.22 = bf16[2,2,2,1,64,1024]{5,4,0,1,2,3:T(8,128)(2,1)S(1)} collective-permute-done((bf16[2,2,2,1,64,1024]{5,4,0,1,2,3:T(8,128)(2,1)S(1)}, bf16[2,2,2,1,64,1024]{5,4,0,1,2,3:T(8,128)(2,1)S(1)}, u32[]{:S(2)}, u32[]{:S(2)}) %collective-permute-start.22) | collective-permute-done | bytes 1048608 | tf_op jit(solution)/shard_map/ppermute | solution.py:37
  169.5 20.4 %collective-permute-done.13 = bf16[2,2,2,1,16,4120]{5,4,2,1,0,3:T(8,128)(2,1)S(1)} collective-permute-done((bf16[2,2,2,1,16,4120]{5,4,2,1,0,3:T(8,128)(2,1)S(1)}, bf16[2,2,2,1,16,4120]{5,4,2,1,0,3:T(8,128)(2,1)S(1)}, u32[]{:S(2)}, u32[]{:S(2)}) %collective-permute-start.13) | collective-permute-done | bytes 1054752 | tf_op jit(solution)/shard_map/ppermute | solution.py:37
  210.0 7.7 pad_maximum_fusion
  217.7 10.6 %convolution_convert_fusion.2 = bf16[512,4120]{0,1:T(8,128)(2,1)S(1)} fusion(bf16[512,1024]{1,0:T(8,128)(2,1)S(1)} %bitcast.933, bf16[1024,4120]{1,0:T(8,128)(2,1)} %bitcast.907), kind=kOutput, calls=%fused_computation.28 | convolution fusion | flops 4322242560 | bytes 13705216 | tf_op jit(solution)/shard_map/dot_general | solution.py:103
  254.3 10.9 %fusion.48 = (f32[2,256,1792]{2,1,0:T(8,128)S(1)}, f32[2,256,1792]{2,1,0:T(8,128)}) fusion(f32[1792]{0:T(1024)S(1)} %copy-done.85, f32[2,256,1792]{2,1,0:T(8,128)} %bitcast.879, f32[2,3,1792]{2,1,0:T(4,128)S(1)} %convert_element_type.591, pred[2,256]{1,0:T(4,128)(4,1)S(1)} %copy-done.114, f32[1792]{0:T(1024)S(1)} %copy-done.83, ...), kind=kLoop, calls=%fused_computation.102 | loop fusion | flops 16515072 | bytes 11090432 | tf_op jit(solution)/shard_map/jvp(jit(silu))/mul | solution.py:132
  286.6 10.6 %fusion.317 = (f32[2,2,4,256]{3,2,1,0:T(4,128)S(1)}, f32[2,2,4,256,1024]{4,3,2,1,0:T(8,128)}) fusion(pred[2,256,1024]{2,1,0:T(8,128)(4,1)} %compare_and_fusion, bf16[2,2,1024,64,1]{2,3,1,0,4:T(8,128)(2,1)} %reshape.1108, bf16[2,256,2,4,64]{1,0,4,3,2:T(2,128)(2,1)} %reshape.1036), kind=kOutput, calls=%fused_computation.641 | convolution fusion | flops 553649152 | bytes 18366464 | tf_op jit(solution)/shard_map/sub | solution.py:295
  297.1 9.6 %fusion.17 = bf16[2,2,4,256,1024]{4,3,2,1,0:T(8,128)(2,1)} fusion(f32[2,2,4,256,1024]{4,3,2,1,0:T(8,128)} %get-tuple-element.172, f32[2,2,4,256]{3,2,1,0:T(4,128)S(1)} %get-tuple-element.171), kind=kLoop, calls=%fused_computation.29 | loop fusion | flops 8388608 | bytes 25182208 | tf_op jit(solution)/shard_map/convert_element_type | solution.py:297
  325.1 10.1 %collective-permute-done.18 = bf16[2,24,64,128]{3,2,1,0:T(8,128)(2,1)S(1)} collective-permute-done((bf16[2,24,64,128]{3,2,1,0:T(8,128)(2,1)S(1)}, bf16[2,24,64,128]{3,2,1,0:T(8,128)(2,1)S(1)}, u32[]{:S(2)}, u32[]{:S(2)}) %collective-permute-start.18) | collective-permute-done | bytes 786464 | tf_op jit(solution)/shard_map/ppermute | solution.py:37
  382.4 10.8 %multiply_reduce_fusion.8 = (f32[1024]{0:T(1024)}, f32[512]{0:T(512)S(1)}, f32[512,1024]{1,0:T(8,128)}) fusion(f32[512,1024]{1,0:T(8,128)} %copy-done.27, f32[512]{0:T(512)S(1)} %fusion.279, f32[1024]{0:T(1024)S(1)} %copy-done.116, bf16[1024,4096]{1,0:T(8,128)(2,1)S(1)} %bitcast.913, f32[512,2048]{1,0:T(8,128)} %get-tuple-element.53, ...), kind=kOutput, calls=%fused_computation.204 | convolution fusion | flops 4302305792 | bytes 20983808 | tf_op jit(solution)/shard_map/dot_general | solution.py:113
  393.2 12.1 %convolution_convert_fusion.1 = bf16[1024,4096]{1,0:T(8,128)(2,1)} fusion(f32[512,2048]{1,0:T(8,128)} %get-tuple-element.53, f32[512,2048]{1,0:T(8,128)} %get-tuple-element.52, f32[512,1024]{1,0:T(8,128)} %copy-done.27, f32[1024]{0:T(1024)S(1)} %copy-done.116, f32[512]{0:T(512)S(1)} %fusion.279), kind=kOutput, calls=%fused_computation.27 | convolution fusion | flops 4304928768 | bytes 18880512 | tf_op jit(solution)/shard_map/dot_general | solution.py:107
  416.8 7.5 multiply_convert_fusion
  445.2 11.6 %fusion.70 = (f32[2,24,256]{2,1,0:T(8,128)}, f32[2,24,256]{2,1,0:T(8,128)}, bf16[2,256,256]{2,1,0:T(8,128)(2,1)S(1)}) fusion(f32[2,24,256]{2,1,0:T(8,128)S(1)} %copy-done.74, f32[2,256,256]{2,1,0:T(8,128)} %fusion.225, pred[2,256,256]{2,1,0:T(8,128)(4,1)} %compare_and_fusion.1, f32[2,24,256,64]{2,3,1,0:T(8,128)S(1)} %bitcast.881, ...), kind=kOutput, calls=%fused_computation.140 | convolution fusion | flops 450469888 | bytes 7405568 | tf_op jit(solution)/shard_map/transpose(jvp(mhts,mhsp->mhtp))/dot_general | solution.py:146
  532.1 15.1 %collective-permute-done.39 = bf16[2,24,64,128]{3,2,1,0:T(8,128)(2,1)} collective-permute-done((bf16[2,24,64,128]{3,2,1,0:T(8,128)(2,1)}, bf16[2,24,64,128]{3,2,1,0:T(8,128)(2,1)}, u32[]{:S(2)}, u32[]{:S(2)}) %collective-permute-start.39) | collective-permute-done | bytes 786464 | tf_op jit(solution)/shard_map/ppermute | solution.py:37
  596.8 11.3 %fusion.90 = (f32[1024]{0:T(1024)S(1)}, f32[512]{0:T(512)S(1)}, bf16[512,1024]{1,0:T(8,128)(2,1)S(1)}, f32[512,1024]{1,0:T(8,128)}) fusion(bf16[2,256,1024]{2,1,0:T(8,128)(2,1)S(1)} %copy-done.11, f32[512]{0:T(512)S(1)} %copy-done.122, f32[1024]{0:T(1024)S(1)} %copy-done.99, bf16[512,4120]{1,0:T(8,128)(2,1)} %constant_dynamic-update-slice_fusion.3, ...), kind=kOutput, calls=%fused_computation.195 | convolution fusion | flops 4324850176 | bytes 16863232 | tf_op jit(solution)/shard_map/dot_general | solution.py:113
  615.0 11.9 %copy.443 = bf16[1024,4120]{1,0:T(8,128)(2,1)} copy(bf16[1024,4120]{0,1:T(8,128)(2,1)} %convolution_convert_fusion) | data formatting | bytes 16875520 | tf_op jit(solution)/shard_map/convert_element_type | solution.py:388
  658.8 14.1 %collective-permute-done.67 = bf16[2,2,2,64,1024]{4,3,0,1,2:T(8,128)(2,1)} collective-permute-done((bf16[2,2,2,64,1024]{4,3,0,1,2:T(8,128)(2,1)}, bf16[2,2,2,64,1024]{4,3,0,1,2:T(8,128)(2,1)}, u32[]{:S(2)}, u32[]{:S(2)}) %collective-permute-start.67) | collective-permute-done | bytes 1048608 | tf_op jit(solution)/shard_map/ppermute | solution.py:37
  677.0 15.2 %collective-permute-done.57 = bf16[2,2,2,64,1024]{4,3,0,1,2:T(8,128)(2,1)} collective-permute-done((bf16[2,2,2,64,1024]{4,3,0,1,2:T(8,128)(2,1)}, bf16[2,2,2,64,1024]{4,3,0,1,2:T(8,128)(2,1)}, u32[]{:S(2)}, u32[]{:S(2)}) %collective-permute-start.57) | collective-permute-done | bytes 1048608 | tf_op jit(solution)/shard_map/ppermute | solution.py:37
  746.0 40.5 %collective-permute-done.53 = bf16[2,2,16,4120]{3,2,0,1:T(8,128)(2,1)S(1)} collective-permute-done((bf16[2,2,16,4120]{3,2,0,1:T(8,128)(2,1)S(1)}, bf16[2,2,16,4120]{3,2,0,1:T(8,128)(2,1)S(1)}, u32[]{:S(2)}, u32[]{:S(2)}) %collective-permute-start.53) | collective-permute-done | bytes 527392 | tf_op jit(solution)/shard_map/ppermute | solution.py:37
  797.4 17.0 %collective-permute-done.63 = bf16[2,2,32,4096]{3,2,0,1:T(8,128)(2,1)S(1)} collective-permute-done((bf16[2,2,32,4096]{3,2,0,1:T(8,128)(2,1)S(1)}, bf16[2,2,32,4096]{3,2,0,1:T(8,128)(2,1)S(1)}, u32[]{:S(2)}, u32[]{:S(2)}) %collective-permute-start.63) | collective-permute-done | bytes 1048608 | tf_op jit(solution)/shard_map/ppermute | solution.py:37
  816.7 10.0 %collective-permute-done.64 = bf16[2,32,4096]{2,1,0:T(8,128)(2,1)S(1)} collective-permute-done((bf16[2,32,4096]{2,1,0:T(8,128)(2,1)S(1)}, bf16[2,32,4096]{2,1,0:T(8,128)(2,1)S(1)}, u32[]{:S(2)}, u32[]{:S(2)}) %collective-permute-start.64) | collective-permute-done | bytes 524320 | tf_op jit(solution)/shard_map/ppermute | solution.py:37
  (775 shorter events, 498.1 us)
Async XLA Ops:
  0.7 57.9 %collective-permute-start.31 = (bf16[1,64,1024]{2,1,0:T(8,128)(2,1)}, bf16[1,64,1024]{2,1,0:T(8,128)(2,1)}, u32[]{:S(2)}, u32[]{:S(2)}) collective-permute-start(bf16[1,64,1024]{2,1,0:T(8,128)(2,1)} %bitcast.954), channel_id=1, source_target_pairs={{0,16},{1,17},{2,18},{3,19},{4,20},{5,21},{6,22},{7,23},{8,24},{9,... | collective-permute-start | bytes 393224 | tf_op jit(solution)/shard_map/ppermute | solution.py:37
  4.8 59.4 %collective-permute-start.26 = (bf16[1,32,4096]{2,1,0:T(8,128)(2,1)}, bf16[1,32,4096]{2,1,0:T(8,128)(2,1)S(1)}, u32[]{:S(2)}, u32[]{:S(2)}) collective-permute-start(bf16[1,32,4096]{2,1,0:T(8,128)(2,1)} %bitcast.947), channel_id=1, source_target_pairs={{0,16},{1,17},{2,18},{3,19},{4,20},{5,21},{6,22},{7,23},{8,24},{9,... | collective-permute-start | bytes 786440 | tf_op jit(solution)/shard_map/ppermute | solution.py:37
  7.4 54.5 %collective-permute-start.10 = (bf16[1,16,4120]{2,1,0:T(8,128)(2,1)S(1)}, bf16[1,16,4120]{2,1,0:T(8,128)(2,1)S(1)}, u32[]{:S(2)}, u32[]{:S(2)}) collective-permute-start(bf16[1,16,4120]{2,1,0:T(8,128)(2,1)S(1)} %get-tuple-element.116), channel_id=1, source_target_pairs={{0,16},{1,17},{2,18},{3,19},{4,20},{5,21},{6,22},{7,23},{8,24},{9,... | collective-permute-start | bytes 395528 | tf_op jit(solution)/shard_map/ppermute | solution.py:37
  10.3 51.6 %collective-permute-start.5 = (bf16[1,16,4120]{2,1,0:T(8,128)(2,1)S(1)}, bf16[1,16,4120]{2,1,0:T(8,128)(2,1)S(1)}, u32[]{:S(2)}, u32[]{:S(2)}) collective-permute-start(bf16[1,16,4120]{2,1,0:T(8,128)(2,1)S(1)} %get-tuple-element.115), channel_id=1, source_target_pairs={{0,16},{1,17},{2,18},{3,19},{4,20},{5,21},{6,22},{7,23},{8,24},{9,... | collective-permute-start | bytes 395528 | tf_op jit(solution)/shard_map/ppermute | solution.py:37
  64.3 32.5 %collective-permute-start.27 = (bf16[2,1,32,4096]{3,2,0,1:T(8,128)(2,1)S(1)}, bf16[2,1,32,4096]{3,2,0,1:T(8,128)(2,1)S(1)}, u32[]{:S(2)}, u32[]{:S(2)}) collective-permute-start(bf16[2,1,32,4096]{3,2,0,1:T(8,128)(2,1)S(1)} %pad_maximum_fusion.21), channel_id=1, source_target_pairs={{0,8},{1,9},{2,10},{3,11},{4,12},{5,13},{6,14},{7,15},{8,0},{9,1},... | collective-permute-start | bytes 1572872 | tf_op jit(solution)/shard_map/ppermute | solution.py:37
  98.8 46.8 %collective-permute-start.34 = (bf16[2,2,2,1,64,1024]{5,4,2,1,0,3:T(8,128)(2,1)S(1)}, bf16[2,2,2,1,64,1024]{5,4,2,1,0,3:T(8,128)(2,1)S(1)}, u32[]{:S(2)}, u32[]{:S(2)}) collective-permute-start(bf16[2,2,2,1,64,1024]{5,4,2,1,0,3:T(8,128)(2,1)S(1)} %fusion.166), channel_id=1, source_target_pairs={{0,4},{1,5},{2,6},{3,7},{4,0},{5,1},{6,2},{7,3},{8,12},{9,13},{10,... | collective-permute-start | bytes 3145736 | tf_op jit(solution)/shard_map/ppermute | solution.py:37
  99.6 68.5 %collective-permute-start.22 = (bf16[2,2,2,1,64,1024]{5,4,0,1,2,3:T(8,128)(2,1)S(1)}, bf16[2,2,2,1,64,1024]{5,4,0,1,2,3:T(8,128)(2,1)S(1)}, u32[]{:S(2)}, u32[]{:S(2)}) collective-permute-start(bf16[2,2,2,1,64,1024]{5,4,0,1,2,3:T(8,128)(2,1)S(1)} %pad_maximum_fusion.13), channel_id=1, source_target_pairs={{0,4},{1,5},{2,6},{3,7},{4,0},{5,1},{6,2},{7,3},{8,12},{9,13},{10,... | collective-permute-start | bytes 3145736 | tf_op jit(solution)/shard_map/ppermute | solution.py:37
  101.4 67.1 %collective-permute-start.8 = (bf16[2,2,2,1,16,4120]{5,4,0,1,2,3:T(8,128)(2,1)S(1)}, bf16[2,2,2,1,16,4120]{5,4,0,1,2,3:T(8,128)(2,1)S(1)}, u32[]{:S(2)}, u32[]{:S(2)}) collective-permute-start(bf16[2,2,2,1,16,4120]{5,4,0,1,2,3:T(8,128)(2,1)S(1)} %pad_maximum_fusion.11), channel_id=1, source_target_pairs={{0,2},{1,3},{2,0},{3,1},{4,6},{5,7},{6,4},{7,5},{8,10},{9,11},{10,... | collective-permute-start | bytes 3164168 | tf_op jit(solution)/shard_map/ppermute | solution.py:37
  107.0 83.0 %collective-permute-start.13 = (bf16[2,2,2,1,16,4120]{5,4,2,1,0,3:T(8,128)(2,1)S(1)}, bf16[2,2,2,1,16,4120]{5,4,2,1,0,3:T(8,128)(2,1)S(1)}, u32[]{:S(2)}, u32[]{:S(2)}) collective-permute-start(bf16[2,2,2,1,16,4120]{5,4,2,1,0,3:T(8,128)(2,1)S(1)} %fusion.165), channel_id=1, source_target_pairs={{0,4},{1,5},{2,6},{3,7},{4,0},{5,1},{6,2},{7,3},{8,12},{9,13},{10,... | collective-permute-start | bytes 3164168 | tf_op jit(solution)/shard_map/ppermute | solution.py:37
  123.5 67.1 %collective-permute-start.29 = (bf16[2,2,2,1,32,4096]{5,4,0,1,2,3:T(8,128)(2,1)S(1)}, bf16[2,2,2,1,32,4096]{5,4,0,1,2,3:T(8,128)(2,1)S(1)}, u32[]{:S(2)}, u32[]{:S(2)}) collective-permute-start(bf16[2,2,2,1,32,4096]{5,4,0,1,2,3:T(8,128)(2,1)S(1)} %pad_maximum_fusion.9), channel_id=1, source_target_pairs={{0,2},{1,3},{2,0},{3,1},{4,6},{5,7},{6,4},{7,5},{8,10},{9,11},{10,... | collective-permute-start | bytes 6291464 | tf_op jit(solution)/shard_map/ppermute | solution.py:37
  146.1 53.8 %collective-permute-start.35 = (bf16[2,2,2,2,1,64,1024]{6,5,3,2,1,0,4:T(8,128)(2,1)S(1)}, bf16[2,2,2,2,1,64,1024]{6,5,3,2,1,0,4:T(8,128)(2,1)S(1)}, u32[]{:S(2)}, u32[]{:S(2)}) collective-permute-start(bf16[2,2,2,2,1,64,1024]{6,5,3,2,1,0,4:T(8,128)(2,1)S(1)} %fusion.120), channel_id=1, source_target_pairs={{0,1},{1,0},{2,3},{3,2},{4,5},{5,4},{6,7},{7,6},{8,9},{9,8},{10,11... | collective-permute-start | bytes 6291464 | tf_op jit(solution)/shard_map/ppermute | solution.py:37
  169.0 38.0 %collective-permute-start.9 = (bf16[2,2,2,2,1,16,4120]{6,5,0,1,2,3,4:T(8,128)(2,1)S(1)}, bf16[2,2,2,2,1,16,4120]{6,5,0,1,2,3,4:T(8,128)(2,1)S(1)}, u32[]{:S(2)}, u32[]{:S(2)}) collective-permute-start(bf16[2,2,2,2,1,16,4120]{6,5,0,1,2,3,4:T(8,128)(2,1)S(1)} %pad_maximum_fusion.6), channel_id=1, source_target_pairs={{0,1},{1,0},{2,3},{3,2},{4,5},{5,4},{6,7},{7,6},{8,9},{9,8},{10,11... | collective-permute-start | bytes 6328328 | tf_op jit(solution)/shard_map/ppermute | solution.py:37
  194.2 161.9 %collective-permute-start.30 = (bf16[2,2,2,2,1,32,4096]{6,5,0,1,2,3,4:T(8,128)(2,1)}, bf16[2,2,2,2,1,32,4096]{6,5,0,1,2,3,4:T(8,128)(2,1)}, u32[]{:S(2)}, u32[]{:S(2)}) collective-permute-start(bf16[2,2,2,2,1,32,4096]{6,5,0,1,2,3,4:T(8,128)(2,1)} %pad_maximum_fusion.4), channel_id=1, source_target_pairs={{0,1},{1,0},{2,3},{3,2},{4,5},{5,4},{6,7},{7,6},{8,9},{9,8},{10,11... | collective-permute-start | bytes 12582920 | tf_op jit(solution)/shard_map/ppermute | solution.py:37
  276.1 37.1 %collective-permute-start.16 = (bf16[2,24,64,128]{3,2,1,0:T(8,128)(2,1)}, bf16[2,24,64,128]{3,2,1,0:T(8,128)(2,1)}, u32[]{:S(2)}, u32[]{:S(2)}) collective-permute-start(bf16[2,24,64,128]{3,2,1,0:T(8,128)(2,1)} %get-tuple-element.167), channel_id=1, source_target_pairs={{0,1},{1,0},{2,3},{3,2},{4,5},{5,4},{6,7},{7,6},{8,9},{9,8},{10,11... | collective-permute-start | bytes 2359304 | tf_op jit(solution)/shard_map/ppermute | solution.py:37
  460.0 63.1 %collective-permute-start.38 = (bf16[2,24,64,128]{3,2,1,0:T(8,128)(2,1)}, bf16[2,24,64,128]{3,2,1,0:T(8,128)(2,1)}, u32[]{:S(2)}, u32[]{:S(2)}) collective-permute-start(bf16[2,24,64,128]{3,2,1,0:T(8,128)(2,1)} %get-tuple-element.177), channel_id=1, source_target_pairs={{0,1},{1,0},{2,3},{3,2},{4,5},{5,4},{6,7},{7,6},{8,9},{9,8},{10,11... | collective-permute-start | bytes 2359304 | tf_op jit(solution)/shard_map/ppermute | solution.py:37
  469.3 173.2 %collective-permute-start.66 = (bf16[2,2,2,2,64,1024]{5,4,0,1,3,2:T(8,128)(2,1)}, bf16[2,2,2,2,64,1024]{5,4,0,1,3,2:T(8,128)(2,1)}, u32[]{:S(2)}, u32[]{:S(2)}) collective-permute-start(bf16[2,2,2,2,64,1024]{5,4,0,1,3,2:T(8,128)(2,1)} %bitcast.874), channel_id=1, source_target_pairs={{0,1},{1,0},{2,3},{3,2},{4,5},{5,4},{6,7},{7,6},{8,9},{9,8},{10,11... | collective-permute-start | bytes 6291464 | tf_op jit(solution)/shard_map/ppermute | solution.py:37
  478.4 244.9 %collective-permute-start.61 = (bf16[2,2,2,2,32,4096]{5,4,0,1,2,3:T(8,128)(2,1)}, bf16[2,2,2,2,32,4096]{5,4,0,1,2,3:T(8,128)(2,1)}, u32[]{:S(2)}, u32[]{:S(2)}) collective-permute-start(bf16[2,2,2,2,32,4096]{5,4,0,1,2,3:T(8,128)(2,1)} %bitcast.871), channel_id=1, source_target_pairs={{0,1},{1,0},{2,3},{3,2},{4,5},{5,4},{6,7},{7,6},{8,9},{9,8},{10,11... | collective-permute-start | bytes 12582920 | tf_op jit(solution)/shard_map/ppermute | solution.py:37
  515.4 131.9 %collective-permute-start.56 = (bf16[2,2,2,2,64,1024]{5,4,0,1,3,2:T(8,128)(2,1)}, bf16[2,2,2,2,64,1024]{5,4,0,1,3,2:T(8,128)(2,1)}, u32[]{:S(2)}, u32[]{:S(2)}) collective-permute-start(bf16[2,2,2,2,64,1024]{5,4,0,1,3,2:T(8,128)(2,1)} %bitcast.873), channel_id=1, source_target_pairs={{0,1},{1,0},{2,3},{3,2},{4,5},{5,4},{6,7},{7,6},{8,9},{9,8},{10,11... | collective-permute-start | bytes 6291464 | tf_op jit(solution)/shard_map/ppermute | solution.py:37
  634.8 71.5 %collective-permute-start.46 = (bf16[2,2,2,2,16,4120]{5,4,3,2,1,0:T(8,128)(2,1)}, bf16[2,2,2,2,16,4120]{5,4,3,2,1,0:T(8,128)(2,1)}, u32[]{:S(2)}, u32[]{:S(2)}) collective-permute-start(bf16[2,2,2,2,16,4120]{5,4,3,2,1,0:T(8,128)(2,1)} %dynamic-slice_bitcast_fusion), channel_id=1, source_target_pairs={{0,1},{1,0},{2,3},{3,2},{4,5},{5,4},{6,7},{7,6},{8,9},{9,8},{10,11... | collective-permute-start | bytes 6328328 | tf_op jit(solution)/shard_map/ppermute | solution.py:37
  651.3 40.9 %collective-permute-start.57 = (bf16[2,2,2,64,1024]{4,3,0,1,2:T(8,128)(2,1)}, bf16[2,2,2,64,1024]{4,3,0,1,2:T(8,128)(2,1)}, u32[]{:S(2)}, u32[]{:S(2)}) collective-permute-start(bf16[2,2,2,64,1024]{4,3,0,1,2:T(8,128)(2,1)} %dynamic-slice_bitcast_fusion.6), channel_id=1, source_target_pairs={{0,4},{1,5},{2,6},{3,7},{4,0},{5,1},{6,2},{7,3},{8,12},{9,13},{10,... | collective-permute-start | bytes 3145736 | tf_op jit(solution)/shard_map/ppermute | solution.py:37
  656.9 52.0 %collective-permute-start.51 = (bf16[2,2,2,2,16,4120]{5,4,0,1,3,2:T(8,128)(2,1)}, bf16[2,2,2,2,16,4120]{5,4,0,1,3,2:T(8,128)(2,1)}, u32[]{:S(2)}, u32[]{:S(2)}) collective-permute-start(bf16[2,2,2,2,16,4120]{5,4,0,1,3,2:T(8,128)(2,1)} %bitcast.872), channel_id=1, source_target_pairs={{0,1},{1,0},{2,3},{3,2},{4,5},{5,4},{6,7},{7,6},{8,9},{9,8},{10,11... | collective-permute-start | bytes 6328328 | tf_op jit(solution)/shard_map/ppermute | solution.py:37
  727.3 68.2 %collective-permute-start.62 = (bf16[2,2,2,32,4096]{4,3,0,1,2:T(8,128)(2,1)S(1)}, bf16[2,2,2,32,4096]{4,3,0,1,2:T(8,128)(2,1)S(1)}, u32[]{:S(2)}, u32[]{:S(2)}) collective-permute-start(bf16[2,2,2,32,4096]{4,3,0,1,2:T(8,128)(2,1)S(1)} %dynamic-slice_bitcast_fusion.1), channel_id=1, source_target_pairs={{0,2},{1,3},{2,0},{3,1},{4,6},{5,7},{6,4},{7,5},{8,10},{9,11},{10,... | collective-permute-start | bytes 6291464 | tf_op jit(solution)/shard_map/ppermute | solution.py:37
  737.1 49.4 %collective-permute-start.53 = (bf16[2,2,16,4120]{3,2,0,1:T(8,128)(2,1)S(1)}, bf16[2,2,16,4120]{3,2,0,1:T(8,128)(2,1)S(1)}, u32[]{:S(2)}, u32[]{:S(2)}) collective-permute-start(bf16[2,2,16,4120]{3,2,0,1:T(8,128)(2,1)S(1)} %dynamic-slice_bitcast_fusion.7), channel_id=1, source_target_pairs={{0,2},{1,3},{2,0},{3,1},{4,6},{5,7},{6,4},{7,5},{8,10},{9,11},{10,... | collective-permute-start | bytes 1582088 | tf_op jit(solution)/shard_map/ppermute | solution.py:37
  745.3 42.3 %collective-permute-start.49 = (bf16[2,16,4120]{2,1,0:T(8,128)(2,1)S(1)}, bf16[2,16,4120]{2,1,0:T(8,128)(2,1)S(1)}, u32[]{:S(2)}, u32[]{:S(2)}) collective-permute-start(bf16[2,16,4120]{2,1,0:T(8,128)(2,1)S(1)} %dynamic-slice_bitcast_fusion.13), channel_id=1, source_target_pairs={{0,8},{1,9},{2,10},{3,11},{4,12},{5,13},{6,14},{7,15},{8,0},{9,1},... | collective-permute-start | bytes 791048 | tf_op jit(solution)/shard_map/ppermute | solution.py:37
  (201 other events, 2544.7 us)

commit v2 on v1

--- a/solution.py
+++ b/solution.py
@@ -212,18 +212,20 @@
     g_gate = small_all[:, cut[3] : cut[4]].reshape(-1).astype(jnp.float32)
     g_ff = small_all[:, cut[4] : cut[5]].reshape(-1).astype(jnp.float32)
 
-    front_shard = jnp.concatenate([q_proj, kv_proj, in_proj], axis=1)
-    halfway = front_shard.shape[0] // 2
-    front_low = spread(front_shard[:halfway], EVERY, count, order_a)
-    front_high = spread(front_shard[halfway:], EVERY, count, order_b)
-    w_front = jnp.concatenate([front_low, front_high], axis=1).reshape(width, -1)
-    close_shard = jnp.concatenate([out_proj, o_proj], axis=0)
-    close_all = spread(close_shard, EVERY, count, order_b)
+    def gather(shard, after):
+        if after is not None:
+            shard = shard + after[:1, :1] * 0
+        return lax.all_gather(shard, EVERY, axis=0, tiled=True)
+
     out_rows = out_proj.shape[0]
-    w_out = close_all[:, :out_rows].reshape(-1, width)
-    w_o = close_all[:, out_rows:].reshape(-1, width)
-    w_gu = spread(gate_up, EVERY, count, order_a).reshape(width, -1)
-    w_down = spread(down_proj, EVERY, count, order_b).reshape(-1, width)
+    both_rows = out_rows + o_proj.shape[0]
+    w_front = gather(jnp.concatenate([q_proj, kv_proj, in_proj], axis=1), None)
+    tall = gather(jnp.concatenate([out_proj, o_proj, down_proj], axis=0), w_front)
+    w_gu = gather(gate_up, tall)
+    tall = tall.reshape(count, -1, width)
+    w_out = tall[:, :out_rows].reshape(-1, width)
+    w_o = tall[:, out_rows:both_rows].reshape(-1, width)
+    w_down = tall[:, both_rows:].reshape(-1, width)
 
     span_len = seq_lengths[0, :, 0] // ctx_count
     local_row = jnp.arange(rows, dtype=jnp.int32)[None, :]
@@ -314,30 +316,46 @@
     layer_out = ((middle + plain_dot(activation_b, w_down)) * alive_row).astype(jnp.bfloat16)
 
     def owned(grad, order):
-        return collect(grad.reshape((count, -1) + grad.shape[1:]), EVERY, count, order)
+        grad = grad.astype(jnp.bfloat16).reshape((count, -1) + grad.shape[1:])
+        return collect(grad, EVERY, count, order).astype(jnp.float32)
 
     back_a = order_a[::-1]
     back_b = order_b[::-1]
     d_out = cotangent.reshape(all_rows, width).astype(jnp.float32) * alive_row
     d_ff_b = d_out.astype(jnp.bfloat16)
-    r_down = owned(left_dot(activation_b, d_ff_b).astype(jnp.bfloat16), back_b)
+    g_down = left_dot(activation_b, d_ff_b).astype(jnp.bfloat16)
     (d_gate_up,) = act_pull(right_dot(d_ff_b, w_down))
     d_gate_up_b = d_gate_up.astype(jnp.bfloat16)
-    r_gu = owned(left_dot(normed_ff_b, d_gate_up_b).astype(jnp.bfloat16), back_a)
+    g_gu = [
+        left_dot(normed_ff_b, d_gate_up_b[:, start : start + width]).astype(jnp.bfloat16)
+        for start in range(0, d_gate_up_b.shape[1], width)
+    ]
     d_mid_part, g_ffgain = ff_pull(right_dot(d_gate_up_b, w_gu))
     d_mid = d_out + d_mid_part
     d_branch_b = d_mid.astype(jnp.bfloat16)
     d_mamba_norm = right_dot(d_branch_b, w_out).reshape(micro, rows, DI)
     d_local, d_cout, d_from, d_state_in, d_gate_z, g_gategain = finish_pull(d_mamba_norm)
     d_end_state = chain_states(d_state_in, decay_wide, "ctx", ctx_count, True)
-    g_close = jnp.concatenate(
-        [
-            left_dot(mamba_norm_b, d_branch_b).astype(jnp.bfloat16).reshape(count, -1, width),
-            left_dot(attended_b, d_branch_b).astype(jnp.bfloat16).reshape(count, -1, width),
-        ],
-        axis=1,
-    )
-    r_close = collect(g_close, EVERY, count, back_b)
+    tall_grads = g_gu + [
+        left_dot(mamba_norm_b, d_branch_b).astype(jnp.bfloat16),
+        left_dot(attended_b, d_branch_b).astype(jnp.bfloat16),
+        g_down,
+    ]
+    tall_grads = [grad.reshape(count, -1, width) for grad in tall_grads]
+    r_tall = lax.psum_scatter(
+        jnp.concatenate(tall_grads, axis=1).reshape(-1, width),
+        EVERY,
+        scatter_dimension=0,
+        tiled=True,
+    ).astype(jnp.float32)
+    gu_rows = gate_up.shape[0]
+    after_gu = gu_rows * len(g_gu)
+    r_gu = jnp.concatenate(
+        [r_tall[k * gu_rows : (k + 1) * gu_rows] for k in range(len(g_gu))], axis=1
+    )
+    r_out = r_tall[after_gu : after_gu + out_rows]
+    r_o = r_tall[after_gu + out_rows : after_gu + both_rows]
+    r_down = r_tall[after_gu + both_rows :]
 
     d_attended_b = right_dot(d_branch_b, w_o).astype(jnp.bfloat16)
     d_att_heads = d_attended_b.reshape(micro, rows, KVH, groups, AD).transpose(0, 2, 3, 1, 4)
@@ -375,22 +393,22 @@
     for step in range(reach):
         hit = row_index == (span_len[:, None] - reach + step)
         d_xbc = d_xbc + jnp.where(hit[..., None], tail_back[:, step : step + 1], 0.0)
-    d_joined_b = jnp.concatenate(
+    d_early_b = jnp.concatenate(
+        [d_query_b, d_keyval, d_gate_z.reshape(all_rows, DI).astype(jnp.bfloat16)], axis=1
+    )
+    d_late_b = jnp.concatenate(
         [
-            d_query_b,
-            d_keyval,
-            d_gate_z.reshape(all_rows, DI).astype(jnp.bfloat16),
             d_xbc.reshape(all_rows, XC).astype(jnp.bfloat16),
             d_raw_step.reshape(all_rows, MH).astype(jnp.bfloat16),
         ],
         axis=1,
     )
-    g_front = left_dot(normed_b, d_joined_b).astype(jnp.bfloat16)
-    g_front = g_front.reshape((count, 2, halfway, -1))
-    r_front = jnp.concatenate(
-        [collect(g_front[:, 0], EVERY, count, back_a), collect(g_front[:, 1], EVERY, count, back_b)],
-        axis=0,
-    ).astype(jnp.float32)
+    half_late = XC // 2
+    r_early = owned(left_dot(normed_b, d_early_b), back_b)
+    r_late_a = owned(left_dot(normed_b, d_late_b[:, :half_late]), back_a)
+    r_late_b = owned(left_dot(normed_b, d_late_b[:, half_late:]), back_b)
+    r_front = jnp.concatenate([r_early, r_late_a, r_late_b], axis=1)
+    d_joined_b = jnp.concatenate([d_early_b, d_late_b], axis=1)
     d_x_part, g_normgain = norm_pull(right_dot(d_joined_b, w_front))
     grad_hidden = (d_mid + d_x_part).astype(jnp.bfloat16)
 
@@ -409,7 +427,6 @@
     heads = jnp.concatenate([g_alog, g_dtbias, g_skip, jnp.zeros((128 - 3 * MH,), jnp.float32)])
     heads = sum_all(heads.reshape(1, 128), EVERY, count)[0]
     own = [r_small[cut[k] : cut[k + 1]] for k in range(5)]
-    r_close = r_close.astype(jnp.float32)
     return (
         layer_out.reshape(hidden.shape),
         grad_hidden.reshape(hidden.shape),
@@ -418,13 +435,13 @@
         own[1].reshape(CONV, -1),
         own[2],
         own[3],
-        r_close[:out_rows],
+        r_out,
         r_front[:, :QD],
         r_front[:, QD : QD + 2 * KD],
-        r_close[out_rows:],
+        r_o,
         own[4],
-        r_gu.astype(jnp.float32),
-        r_down.astype(jnp.float32),
+        r_gu,
+        r_down,
         heads[:MH],
         heads[MH : 2 * MH],
         heads[2 * MH : 3 * MH],

time: 849 us -> 729 us (0.86)
  other arithmetic: 137 us -> 92.2 us
  waiting for transfers between devices: 291 us -> 248 us
  starting transfers between devices: 86.2 us -> 44.9 us
  between operations: 6.73 us -> 20.3 us
  local copies, waits for them, and re-layouts: 153 us -> 140 us
  matrix products: 164 us -> 173 us
    ppermute x74 -> x39, waiting for transfers between devices: 291 us -> 116 us  [swap_with(): return lax.ppermute(block, axes, [(i, i ^ bit) for i in range(count)])]
    all_gather x0 -> x3, waiting for transfers between devices: none -> 132 us  [gather(): return lax.all_gather(shard, EVERY, axis=0, tiled=True)]
    ppermute x74 -> x39, starting transfers between devices: 82.4 us -> 40.9 us  [swap_with(): return lax.ppermute(block, axes, [(i, i ^ bit) for i in range(count)])]
    another operation x69 -> x14, other arithmetic: 26 us -> 1.57 us  [spread(): jnp.stack([jnp.where(upper, other, held), jnp.where(upper, held, other)])]
    convert_element_type x24 -> x14, other arithmetic: 22.1 us -> 8.02 us  [collect(): (kept.astype(jnp.float32) + other.astype(jnp.float32)).astype(parts.dtype)]
    slice x6 -> x11, local copies, waits for them, and re-layouts: 9.26 us -> 19.2 us  [the longest x1 5.99 us: body(): w_down = tall[:, both_rows:].reshape(-1, width)]
    concatenate x2 -> x3, other arithmetic: 12.6 us -> 3.36 us  [the longest x1 1.74 us: body(): w_front = gather(jnp.concatenate([q_proj, kv_proj, in_proj], axis=1), None)]
    convert_element_type x1, local copies, waits for them, and re-layouts: 11.9 us -> 3.05 us  [owned(): grad = grad.astype(jnp.bfloat16).reshape((count, -1) + grad.shape[1:])]
  transfers between devices with their start and end apart: 76 -> 45, of which waited for: 38 -> 21; matrix products, arithmetic and copies ran while one was open for 41% -> 44% of each run, Pallas kernels for 0% -> 0%
where the time goes in v2:
time: 729 us; the launch traced here: 719 us
  waiting for transfers between devices  248 us (34%)
  matrix products  173 us (24%)
  local copies, waits for them, and re-layouts  140 us (19%)
  other arithmetic  92.2 us (13%)
  starting transfers between devices  44.9 us (6%)
  between operations  20.3 us (3%)
    all_gather x3, waiting for transfers between devices, gather(): return lax.all_gather(shard, EVERY, axis=0, tiled=True)  132 us
    ppermute x39, waiting for transfers between devices, swap_with(): return lax.ppermute(block, axes, [(i, i ^ bit) for i in range(count)])  116 us
    ppermute x39, starting transfers between devices, swap_with(): return lax.ppermute(block, axes, [(i, i ^ bit) for i in range(count)])  40.9 us
    dot_general x5, matrix products, right_dot(): lax.dot_general(first_arg, second_arg, (((1,), (1,)), ((), ())), preferre...  32.9 us
    unnamed x285, local copies, waits for them, and re-layouts  29 us
    dot_general x10, matrix products, left_dot(): lax.dot_general(first_arg, second_arg, (((0,), (0,)), ((), ())), preferre...  27.2 us
    dot_general x5, matrix products, plain_dot(): return jnp.dot(first_arg, second_arg, preferred_element_type=jnp.float32)  24.1 us
    dot_general x3, matrix products, mamba_local(): jnp.einsum('mhts,mhsp->mhtp', mixing, scaled)  21.5 us
  transfers between devices with their start and end apart: 45, of which 21 were waited for; matrix products, arithmetic and copies ran while one was open for 44% of the time, Pallas kernels for 0%

profile of v2, /device:TPU:0, one launch (start us, length us, event | category | flops | bytes accessed | tf_op | source)
XLA Modules:
  0.0 718.6 jit_solution(4560974441521731508)
XLA Ops:
  9.1 83.5 %all-gather.4.cloned.1.call-done = bf16[1024,4120]{1,0:T(8,128)(2,1)} async-done(((bf16[32,4120]{1,0:T(8,128)(2,1)}), bf16[1024,4120]{1,0:T(8,128)(2,1)}) %all-gather.4.cloned.1.call-update) | async-done | bytes 8437776 | tf_op jit(solution)/shard_map/all_gather | solution.py:218
  123.8 48.6 %all-gather.6.cloned.1.call-done = bf16[4096,1024]{1,0:T(8,128)(2,1)} async-done(((bf16[128,1024]{1,0:T(8,128)(2,1)}), bf16[4096,1024]{1,0:T(8,128)(2,1)}) %all-gather.6.cloned.1.call-update) | async-done | bytes 8388624 | tf_op jit(solution)/shard_map/all_gather | solution.py:218
  179.9 10.7 %convolution_convert_fusion = bf16[512,4120]{0,1:T(8,128)(2,1)S(1)} fusion(bf16[512,1024]{1,0:T(8,128)(2,1)S(1)} %fusion.83, bf16[1024,4120]{1,0:T(8,128)(2,1)} %all-gather.4.cloned.1.call-done), kind=kOutput, calls=%fused_computation.22 | convolution fusion | flops 4322242560 | bytes 13705216 | tf_op jit(solution)/shard_map/dot_general | solution.py:103
  219.7 11.1 %fusion.43 = (f32[2,256,1792]{2,1,0:T(8,128)S(1)}, f32[2,256,1792]{2,1,0:T(8,128)}) fusion(f32[1792]{0:T(1024)S(1)} %copy-done.72, f32[2,256,1792]{2,1,0:T(8,128)} %bitcast.567, f32[2,3,1792]{2,1,0:T(4,128)S(1)} %convert_element_type.479, pred[2,256]{1,0:T(4,128)(4,1)S(1)} %copy-done.104, f32[1792]{0:T(1024)S(1)} %copy-done.74, ...), kind=kLoop, calls=%fused_computation.74 | loop fusion | flops 16515072 | bytes 11090432 | tf_op jit(solution)/shard_map/jvp(jit(silu))/mul | solution.py:132
  252.0 10.6 %fusion.292 = (f32[2,2,4,256]{3,2,1,0:T(4,128)S(1)}, f32[2,2,4,256,1024]{4,3,2,1,0:T(8,128)}) fusion(pred[2,256,1024]{2,1,0:T(8,128)(4,1)} %compare_and_fusion, bf16[2,2,1024,64,1]{2,3,1,0,4:T(8,128)(2,1)} %reshape.1060, bf16[2,256,2,4,64]{1,0,4,3,2:T(2,128)(2,1)} %reshape.992), kind=kOutput, calls=%fused_computation.521 | convolution fusion | flops 553649152 | bytes 18366464 | tf_op jit(solution)/shard_map/sub | solution.py:297
  262.5 9.7 %fusion.16 = bf16[2,2,4,256,1024]{4,3,2,1,0:T(8,128)(2,1)} fusion(f32[2,2,4,256,1024]{4,3,2,1,0:T(8,128)} %get-tuple-element.129, f32[2,2,4,256]{3,2,1,0:T(4,128)S(1)} %get-tuple-element.128), kind=kLoop, calls=%fused_computation.23 | loop fusion | flops 8388608 | bytes 25182208 | tf_op jit(solution)/shard_map/convert_element_type | solution.py:299
  283.6 6.0 fusion.165
  291.2 10.1 %collective-permute-done.8 = bf16[2,24,64,128]{3,2,1,0:T(8,128)(2,1)S(1)} collective-permute-done((bf16[2,24,64,128]{3,2,1,0:T(8,128)(2,1)S(1)}, bf16[2,24,64,128]{3,2,1,0:T(8,128)(2,1)S(1)}, u32[]{:S(2)}, u32[]{:S(2)}) %collective-permute-start.8) | collective-permute-done | bytes 786464 | tf_op jit(solution)/shard_map/ppermute | solution.py:37
  322.6 6.0 slice.295
  332.8 7.4 %fusion.27 = f32[512,4096]{1,0:T(8,128)S(1)} fusion(bf16[512,1024]{1,0:T(8,128)(2,1)} %multiply_convert_fusion.5, bf16[1024,4096]{1,0:T(8,128)(2,1)} %all-gather.8.cloned.1.call-done), kind=kOutput, calls=%fused_computation.36 | convolution fusion | flops 4299161600 | bytes 17825792 | tf_op jit(solution)/shard_map/dot_general | solution.py:103
  340.2 6.1 fusion.180
  359.9 7.3 %multiply_reduce_fusion.8 = (f32[1024]{0:T(1024)S(1)}, f32[512]{0:T(512)S(1)}, f32[512,1024]{1,0:T(8,128)S(1)}) fusion(f32[512,1024]{1,0:T(8,128)S(1)} %get-tuple-element.131, f32[512]{0:T(512)S(1)} %fusion.256, f32[1024]{0:T(1024)S(1)} %copy-done.88, bf16[512,4096]{1,0:T(8,128)(2,1)S(1)} %add_convert_fusion, ...), kind=kOutput, calls=%fused_computation.153 | convolution fusion | flops 4298111488 | bytes 16789504 | tf_op jit(solution)/shard_map/dot_general | solution.py:113
  380.3 9.4 %multiply_convert_fusion = bf16[2,2,4,256,1024]{4,3,2,1,0:T(8,128)(2,1)} fusion(f32[2,2,4,256]{3,2,1,0:T(4,128)S(1)} %multiply_reduce_fusion.12, f32[2,2,4,256,1024]{4,3,2,1,0:T(8,128)} %get-tuple-element.129, f32[2,2,4,256]{3,2,1,0:T(4,128)S(1)} %get-tuple-element.128, bf16[2,256,2,4,64]{1,4,3,2,0:T(8,128)(2,1)S(1)} %copy.195, ...), kind=kOutput, calls=%fused_computation.4 | convolution fusion | flops 553648128 | bytes 26247168 | tf_op jit(solution)/shard_map/mgjtd,mgsd->mgjts/dot_general | solution.py:362
  427.5 6.6 multiply_reduce_fusion.5
  440.3 11.2 %fusion.65 = (f32[2,24,256]{2,1,0:T(8,128)}, f32[2,24,256]{2,1,0:T(8,128)}, bf16[2,256,256]{2,1,0:T(8,128)(2,1)S(1)}) fusion(f32[2,24,256]{2,1,0:T(8,128)S(1)} %copy-done.67, f32[2,256,256]{2,1,0:T(8,128)} %fusion.204, pred[2,256,256]{2,1,0:T(8,128)(4,1)S(1)} %copy-done.69, f32[2,24,256,64]{2,3,1,0:T(8,128)S(1)} %bitcast.569, ...), kind=kOutput, calls=%fused_computation.112 | convolution fusion | flops 450469888 | bytes 7405568 | tf_op jit(solution)/shard_map/transpose(jvp(mhts,mhsp->mhtp))/dot_general | solution.py:146
  456.5 7.1 fusion.116
  489.4 13.1 %collective-permute-done.12 = bf16[2,256,256]{2,1,0:T(8,128)(2,1)S(1)} collective-permute-done((bf16[2,256,256]{2,1,0:T(8,128)(2,1)S(1)}, bf16[2,256,256]{2,1,0:T(8,128)(2,1)S(1)}, u32[]{:S(2)}, u32[]{:S(2)}) %collective-permute-start.12) | collective-permute-done | bytes 262176 | tf_op jit(solution)/shard_map/ppermute | solution.py:37
  510.7 24.5 %collective-permute-done.14 = bf16[2,24,64,128]{3,2,1,0:T(8,128)(2,1)S(1)} collective-permute-done((bf16[2,24,64,128]{3,2,1,0:T(8,128)(2,1)S(1)}, bf16[2,24,64,128]{3,2,1,0:T(8,128)(2,1)S(1)}, u32[]{:S(2)}, u32[]{:S(2)}) %collective-permute-start.14) | collective-permute-done | bytes 786464 | tf_op jit(solution)/shard_map/ppermute | solution.py:37
  537.4 5.7 fusion.50
  559.3 5.6 fusion.278
  588.2 11.2 %fusion.84 = (f32[1024]{0:T(1024)S(1)}, f32[512]{0:T(512)S(1)}, f32[512,1024]{1,0:T(8,128)}) fusion(bf16[2,256,1024]{2,1,0:T(8,128)(2,1)S(1)} %copy-done.7, f32[512]{0:T(512)S(1)} %copy-done.96, f32[1024]{0:T(1024)S(1)} %copy-done.87, bf16[512,4120]{1,0:T(8,128)(2,1)} %constant_dynamic-update-slice_fusion, bf16[1024,4120]{1,0:T(8,128)(2,1)} %all-gather.4.cloned.1.call-done), kind=kOutput, calls=%fused_computation.149 | convolution fusion | flops 4323801600 | bytes 15814656 | tf_op jit(solution)/shard_map/dot_general | solution.py:113
  647.0 26.1 %collective-permute-done.28 = bf16[2,2,32,896]{3,2,0,1:T(8,128)(2,1)S(1)} collective-permute-done((bf16[2,2,32,896]{3,2,0,1:T(8,128)(2,1)S(1)}, bf16[2,2,32,896]{3,2,0,1:T(8,128)(2,1)S(1)}, u32[]{:S(2)}, u32[]{:S(2)}) %collective-permute-start.28) | collective-permute-done | bytes 229408 | tf_op jit(solution)/shard_map/ppermute | solution.py:37
  681.4 7.3 %collective-permute-done.23 = bf16[2,2,32,2304]{3,2,0,1:T(8,128)(2,1)S(1)} collective-permute-done((bf16[2,2,32,2304]{3,2,0,1:T(8,128)(2,1)S(1)}, bf16[2,2,32,2304]{3,2,0,1:T(8,128)(2,1)S(1)}, u32[]{:S(2)}, u32[]{:S(2)}) %collective-permute-start.23) | collective-permute-done | bytes 589856 | tf_op jit(solution)/shard_map/ppermute | solution.py:37
  691.1 5.5 collective-permute-done.24
  (612 shorter events, 348.0 us)
Async XLA Ops:
  7.2 85.4 %all-gather.4.cloned.1.call-start = ((), (), s32[]{:S(2)}) async-start(), calls=%async_computation.1 | async-start | bytes 8921088 | tf_op jit(solution)/shard_map/all_gather | solution.py:218
  9.0 163.3 %all-gather.6.cloned.1.call-start = ((), (), s32[]{:S(2)}) async-start(), calls=%async_computation.2 | async-start | bytes 8650752 | tf_op jit(solution)/shard_map/all_gather | solution.py:218
  96.2 236.6 %all-gather.8.cloned.1.call-start = ((), (), s32[]{:S(2)}) async-start(), calls=%async_computation.3 | async-start | bytes 8650752 | tf_op jit(solution)/shard_map/all_gather | solution.py:218
  99.8 8.4 %collective-permute-start = (bf16[1,4,128]{2,1,0:T(4,128)(2,1)S(1)}, bf16[1,4,128]{2,1,0:T(4,128)(2,1)S(1)}, u32[]{:S(2)}, u32[]{:S(2)}) collective-permute-start(bf16[1,4,128]{2,1,0:T(4,128)(2,1)S(1)} %bitcast.654), channel_id=1, source_target_pairs={{0,16},{1,17},{2,18},{3,19},{4,20},{5,21},{6,22},{7,23},{8,24},{9,... | collective-permute-start | bytes 3080 | tf_op jit(solution)/shard_map/ppermute | solution.py:37
  174.9 530.6 %reduce-scatter.2.cloned.1.call-start = ((), (), s32[]{:S(2)}) async-start(), calls=%async_computation.4 | async-start | bytes 17301504 | tf_op jit(solution)/shard_map/reduce_scatter | solution.py:345
  199.6 37.5 %collective-permute-start.9 = (bf16[1,2,256,256]{3,2,1,0:T(8,128)(2,1)}, bf16[1,2,256,256]{3,2,1,0:T(8,128)(2,1)S(1)}, u32[]{:S(2)}, u32[]{:S(2)}) collective-permute-start(bf16[1,2,256,256]{3,2,1,0:T(8,128)(2,1)} %bitcast.173), channel_id=1, source_target_pairs={{0,2},{1,3},{2,0},{3,1},{4,6},{5,7},{6,4},{7,5},{8,10},{9,11},{10,... | collective-permute-start | bytes 786440 | tf_op jit(solution)/shard_map/ppermute | solution.py:37
  204.9 14.0 %collective-permute-start.7 = (f32[2,24,1,1]{1,0,3,2:T(2,128)S(1)}, f32[2,24,1,1]{1,0,3,2:T(2,128)S(1)}, u32[]{:S(2)}, u32[]{:S(2)}) collective-permute-start(f32[2,24,1,1]{1,0,3,2:T(2,128)S(1)} %get-tuple-element.107), channel_id=1, source_target_pairs={{0,1},{1,0},{2,3},{3,2},{4,5},{5,4},{6,7},{7,6},{8,9},{9,8},{10,11... | collective-permute-start | bytes 584 | tf_op jit(solution)/shard_map/ppermute | solution.py:37
  241.8 37.0 %collective-permute-start.6 = (bf16[2,24,64,128]{3,2,1,0:T(8,128)(2,1)}, bf16[2,24,64,128]{3,2,1,0:T(8,128)(2,1)}, u32[]{:S(2)}, u32[]{:S(2)}) collective-permute-start(bf16[2,24,64,128]{3,2,1,0:T(8,128)(2,1)} %get-tuple-element.124), channel_id=1, source_target_pairs={{0,1},{1,0},{2,3},{3,2},{4,5},{5,4},{6,7},{7,6},{8,9},{9,8},{10,11... | collective-permute-start | bytes 2359304 | tf_op jit(solution)/shard_map/ppermute | solution.py:37
  280.9 20.5 %collective-permute-start.8 = (bf16[2,24,64,128]{3,2,1,0:T(8,128)(2,1)S(1)}, bf16[2,24,64,128]{3,2,1,0:T(8,128)(2,1)S(1)}, u32[]{:S(2)}, u32[]{:S(2)}) collective-permute-start(bf16[2,24,64,128]{3,2,1,0:T(8,128)(2,1)S(1)} %fusion.94), channel_id=1, source_target_pairs={{0,2},{1,3},{2,0},{3,1},{4,6},{5,7},{6,4},{7,5},{8,10},{9,11},{10,... | collective-permute-start | bytes 2359304 | tf_op jit(solution)/shard_map/ppermute | solution.py:37
  427.5 56.7 %collective-permute-start.11 = (bf16[2,2,256,256]{3,2,1,0:T(8,128)(2,1)}, bf16[2,2,256,256]{3,2,1,0:T(8,128)(2,1)}, u32[]{:S(2)}, u32[]{:S(2)}) collective-permute-start(bf16[2,2,256,256]{3,2,1,0:T(8,128)(2,1)} %bitcast.626), channel_id=1, source_target_pairs={{0,1},{1,0},{2,3},{3,2},{4,5},{5,4},{6,7},{7,6},{8,9},{9,8},{10,11... | collective-permute-start | bytes 1572872 | tf_op jit(solution)/shard_map/ppermute | solution.py:37
  474.1 13.4 %collective-permute-start.13 = (bf16[2,24,64,128]{3,2,1,0:T(8,128)(2,1)}, bf16[2,24,64,128]{3,2,1,0:T(8,128)(2,1)}, u32[]{:S(2)}, u32[]{:S(2)}) collective-permute-start(bf16[2,24,64,128]{3,2,1,0:T(8,128)(2,1)} %get-tuple-element.134), channel_id=1, source_target_pairs={{0,1},{1,0},{2,3},{3,2},{4,5},{5,4},{6,7},{7,6},{8,9},{9,8},{10,11... | collective-permute-start | bytes 2359304 | tf_op jit(solution)/shard_map/ppermute | solution.py:37
  485.6 16.9 %collective-permute-start.12 = (bf16[2,256,256]{2,1,0:T(8,128)(2,1)S(1)}, bf16[2,256,256]{2,1,0:T(8,128)(2,1)S(1)}, u32[]{:S(2)}, u32[]{:S(2)}) collective-permute-start(bf16[2,256,256]{2,1,0:T(8,128)(2,1)S(1)} %dynamic-slice_bitcast_fusion.7), channel_id=1, source_target_pairs={{0,2},{1,3},{2,0},{3,1},{4,6},{5,7},{6,4},{7,5},{8,10},{9,11},{10,... | collective-permute-start | bytes 786440 | tf_op jit(solution)/shard_map/ppermute | solution.py:37
  489.1 46.1 %collective-permute-start.14 = (bf16[2,24,64,128]{3,2,1,0:T(8,128)(2,1)S(1)}, bf16[2,24,64,128]{3,2,1,0:T(8,128)(2,1)S(1)}, u32[]{:S(2)}, u32[]{:S(2)}) collective-permute-start(bf16[2,24,64,128]{3,2,1,0:T(8,128)(2,1)S(1)} %fusion.97), channel_id=1, source_target_pairs={{0,2},{1,3},{2,0},{3,1},{4,6},{5,7},{6,4},{7,5},{8,10},{9,11},{10,... | collective-permute-start | bytes 2359304 | tf_op jit(solution)/shard_map/ppermute | solution.py:37
  508.6 123.2 %collective-permute-start.21 = (bf16[2,2,2,2,32,2304]{5,4,0,1,3,2:T(8,128)(2,1)}, bf16[2,2,2,2,32,2304]{5,4,0,1,3,2:T(8,128)(2,1)}, u32[]{:S(2)}, u32[]{:S(2)}) collective-permute-start(bf16[2,2,2,2,32,2304]{5,4,0,1,3,2:T(8,128)(2,1)} %bitcast.561), channel_id=1, source_target_pairs={{0,1},{1,0},{2,3},{3,2},{4,5},{5,4},{6,7},{7,6},{8,9},{9,8},{10,11... | collective-permute-start | bytes 7077896 | tf_op jit(solution)/shard_map/ppermute | solution.py:37
  555.8 9.1 %collective-permute-start.36 = (f32[1,128]{1,0:T(1,128)S(1)}, f32[1,128]{1,0:T(1,128)S(1)}, u32[]{:S(2)}, u32[]{:S(2)}) collective-permute-start(f32[1,128]{1,0:T(1,128)S(1)} %maximum_bitcast_fusion.1), channel_id=1, source_target_pairs={{0,1},{1,0},{2,3},{3,2},{4,5},{5,4},{6,7},{7,6},{8,9},{9,8},{10,11... | collective-permute-start | bytes 1544 | tf_op jit(solution)/shard_map/ppermute | solution.py:37
  614.2 14.4 %collective-permute-start.31 = (bf16[2,2,2,2,32,920]{5,4,3,2,1,0:T(8,128)(2,1)}, bf16[2,2,2,2,32,920]{5,4,3,2,1,0:T(8,128)(2,1)}, u32[]{:S(2)}, u32[]{:S(2)}) collective-permute-start(bf16[2,2,2,2,32,920]{5,4,3,2,1,0:T(8,128)(2,1)} %dynamic-slice_bitcast_fusion.1), channel_id=1, source_target_pairs={{0,1},{1,0},{2,3},{3,2},{4,5},{5,4},{6,7},{7,6},{8,9},{9,8},{10,11... | collective-permute-start | bytes 2826248 | tf_op jit(solution)/shard_map/ppermute | solution.py:37
  628.0 11.2 %collective-permute-start.27 = (bf16[2,2,2,32,896]{4,3,0,1,2:T(8,128)(2,1)S(1)}, bf16[2,2,2,32,896]{4,3,0,1,2:T(8,128)(2,1)S(1)}, u32[]{:S(2)}, u32[]{:S(2)}) collective-permute-start(bf16[2,2,2,32,896]{4,3,0,1,2:T(8,128)(2,1)S(1)} %dynamic-slice_bitcast_fusion.4), channel_id=1, source_target_pairs={{0,2},{1,3},{2,0},{3,1},{4,6},{5,7},{6,4},{7,5},{8,10},{9,11},{10,... | collective-permute-start | bytes 1376264 | tf_op jit(solution)/shard_map/ppermute | solution.py:37
  630.3 14.9 %collective-permute-start.32 = (bf16[2,2,2,32,920]{4,3,2,1,0:T(8,128)(2,1)S(1)}, bf16[2,2,2,32,920]{4,3,2,1,0:T(8,128)(2,1)S(1)}, u32[]{:S(2)}, u32[]{:S(2)}) collective-permute-start(bf16[2,2,2,32,920]{4,3,2,1,0:T(8,128)(2,1)S(1)} %dynamic-slice_bitcast_fusion.3), channel_id=1, source_target_pairs={{0,4},{1,5},{2,6},{3,7},{4,0},{5,1},{6,2},{7,3},{8,12},{9,13},{10,... | collective-permute-start | bytes 1413128 | tf_op jit(solution)/shard_map/ppermute | solution.py:37
  634.2 40.8 %collective-permute-start.22 = (bf16[2,2,2,32,2304]{4,3,0,1,2:T(8,128)(2,1)S(1)}, bf16[2,2,2,32,2304]{4,3,0,1,2:T(8,128)(2,1)S(1)}, u32[]{:S(2)}, u32[]{:S(2)}) collective-permute-start(bf16[2,2,2,32,2304]{4,3,0,1,2:T(8,128)(2,1)S(1)} %dynamic-slice_bitcast_fusion), channel_id=1, source_target_pairs={{0,4},{1,5},{2,6},{3,7},{4,0},{5,1},{6,2},{7,3},{8,12},{9,13},{10,... | collective-permute-start | bytes 3538952 | tf_op jit(solution)/shard_map/ppermute | solution.py:37
  639.3 33.8 %collective-permute-start.28 = (bf16[2,2,32,896]{3,2,0,1:T(8,128)(2,1)S(1)}, bf16[2,2,32,896]{3,2,0,1:T(8,128)(2,1)S(1)}, u32[]{:S(2)}, u32[]{:S(2)}) collective-permute-start(bf16[2,2,32,896]{3,2,0,1:T(8,128)(2,1)S(1)} %dynamic-slice_bitcast_fusion.8), channel_id=1, source_target_pairs={{0,4},{1,5},{2,6},{3,7},{4,0},{5,1},{6,2},{7,3},{8,12},{9,13},{10,... | collective-permute-start | bytes 688136 | tf_op jit(solution)/shard_map/ppermute | solution.py:37
  645.5 29.3 %collective-permute-start.33 = (bf16[2,2,32,920]{3,2,1,0:T(8,128)(2,1)S(1)}, bf16[2,2,32,920]{3,2,1,0:T(8,128)(2,1)S(1)}, u32[]{:S(2)}, u32[]{:S(2)}) collective-permute-start(bf16[2,2,32,920]{3,2,1,0:T(8,128)(2,1)S(1)} %dynamic-slice_bitcast_fusion.6), channel_id=1, source_target_pairs={{0,2},{1,3},{2,0},{3,1},{4,6},{5,7},{6,4},{7,5},{8,10},{9,11},{10,... | collective-permute-start | bytes 706568 | tf_op jit(solution)/shard_map/ppermute | solution.py:37
  675.3 13.4 %collective-permute-start.23 = (bf16[2,2,32,2304]{3,2,0,1:T(8,128)(2,1)S(1)}, bf16[2,2,32,2304]{3,2,0,1:T(8,128)(2,1)S(1)}, u32[]{:S(2)}, u32[]{:S(2)}) collective-permute-start(bf16[2,2,32,2304]{3,2,0,1:T(8,128)(2,1)S(1)} %dynamic-slice_bitcast_fusion.2), channel_id=1, source_target_pairs={{0,2},{1,3},{2,0},{3,1},{4,6},{5,7},{6,4},{7,5},{8,10},{9,11},{10,... | collective-permute-start | bytes 1769480 | tf_op jit(solution)/shard_map/ppermute | solution.py:37
  679.8 11.3 %collective-permute-start.30 = (bf16[32,896]{1,0:T(8,128)(2,1)S(1)}, bf16[32,896]{1,0:T(8,128)(2,1)S(1)}, u32[]{:S(2)}, u32[]{:S(2)}) collective-permute-start(bf16[32,896]{1,0:T(8,128)(2,1)S(1)} %dynamic-slice_bitcast_fusion.13), channel_id=1, source_target_pairs={{0,16},{1,17},{2,18},{3,19},{4,20},{5,21},{6,22},{7,23},{8,24},{9,... | collective-permute-start | bytes 172040 | tf_op jit(solution)/shard_map/ppermute | solution.py:37
  689.3 9.8 %collective-permute-start.35 = (bf16[32,920]{1,0:T(8,128)(2,1)S(1)}, bf16[32,920]{1,0:T(8,128)(2,1)S(1)}, u32[]{:S(2)}, u32[]{:S(2)}) collective-permute-start(bf16[32,920]{1,0:T(8,128)(2,1)S(1)} %dynamic-slice_bitcast_fusion.12), channel_id=1, source_target_pairs={{0,16},{1,17},{2,18},{3,19},{4,20},{5,21},{6,22},{7,23},{8,24},{9,... | collective-permute-start | bytes 176648 | tf_op jit(solution)/shard_map/ppermute | solution.py:37
  (151 other events, 1970.5 us)
Sparse Core Ops, SparseCore 0:
  11.5 81.0 all-gather.3
  96.4 75.9 all-gather.5
  175.8 77.3 all-gather.7
  405.9 207.8 reduce-scatter.1
